TPU v7x, 256 devices: a whole 4x4x8 slice. The times are simulated.
256 devices in a mesh: gz: 32 (over z_lo, y, x), gy: 8 (over z_hi, core).
Axes of the slice: x: 4, y: 4, z: 8 (z_hi: 4, z_lo: 2; z = z_hi * 2 + z_lo), core: 2. Of those that a mesh axis runs over, the one named last changes fastest.
Arguments:
- fodf: float32 [192, 64, 64, 128], P(None, 'gy', 'gz'), may hold values from 0 to 21, as said below
- directions: float32 [3, 192], replicated, may hold values from -1 to 1, as said below
- signs: int32 [3, 192], replicated, may hold values from -1 to 1, as said below
Outputs:
- enhanced: float32 [192, 64, 64, 128], P(None, 'gy', 'gz')
Inputs may be any that keep to these rules, and one draw needn't show every extreme that they name: `fodf`: Non-negative densities. `directions`: unit vectors; orientation k + 96 is the antipode of orientation k; no component is zero. `signs`: each sign is the sign of the matching component of directions; along each axis exactly 96 orientations have sign 1.
All inputs are finite; a program needn't handle non-finite values.
Results may differ from a plain program's by a relative error of at most 0.0003.
Values sent between devices are 32-bit elements; how exact they have to be, the bound alone decides.
A program may use at most 64 MiB of HBM per device.

v0:
```python
import math

import jax
import jax.numpy as jnp
from jax import lax
from jax.sharding import PartitionSpec as P

LMAX = 8
ITERS = 4


TIME_STEP = 0.5
DIFFUSION = 0.02


def padded(value, sides, width):
    edges = {}
    for axis, dim in sides:
        peers, length = (lax.axis_size(axis), value.shape[dim])
        up = [(i, (i + 1) % peers) for i in range(peers - 1)]
        last = lax.slice_in_dim(value, length - width, length, axis=dim)
        initial = lax.slice_in_dim(value, 0, width, axis=dim)
        edges[dim] = (
            lax.ppermute(last, axis, up),
            lax.ppermute(initial, axis, [(b, a) for a, b in up]),
        )
    done = []
    for _, dim in sides:
        low, high = edges[dim]
        around = [(width, width) if d in done else (0, 0) for d in range(value.ndim)]
        value = jnp.concatenate([jnp.pad(low, around), value, jnp.pad(high, around)], axis=dim)
        done.append(dim)
    return value


def double_factorial(value):
    result = 1
    while value > 1:
        result = result * value
        value = value - 2
    return result


def harmonic_rows(directions):
    along_x, along_y, along_z = (directions[0], directions[1], directions[2])
    cosines = [jnp.ones_like(along_x)]
    sines = [jnp.zeros_like(along_x)]
    for order in range(1, LMAX + 1):
        cosines.append(cosines[-1] * along_x - sines[-1] * along_y)
        sines.append(cosines[-2] * along_y + sines[-1] * along_x)
    legendre = {}
    for order in range(LMAX + 1):
        legendre[order, order] = double_factorial(2 * order - 1) * jnp.ones_like(along_z)
        if order + 1 <= LMAX:
            legendre[order + 1, order] = (2 * order + 1) * along_z * legendre[order, order]
        for degree in range(order + 2, LMAX + 1):
            legendre[degree, order] = (
                (2 * degree - 1) * along_z * legendre[degree - 1, order]
                - (degree + order - 1) * legendre[degree - 2, order]
            ) / (degree - order)
    basis_rows = []
    eigen_values = []
    for degree in range(0, LMAX + 1, 2):
        for order in range(degree + 1):
            weight_norm = math.sqrt(
                (2 * degree + 1) * math.factorial(degree - order) / math.factorial(degree + order)
            )
            basis_rows.append(weight_norm * legendre[degree, order] * cosines[order])
            eigen_values.append(-float(degree * (degree + 1)))
            if order > 0:
                basis_rows.append(weight_norm * legendre[degree, order] * sines[order])
                eigen_values.append(-float(degree * (degree + 1)))
    return (jnp.stack(basis_rows, 0), jnp.array(eigen_values, dtype=directions.dtype))


def angular_maps(directions):
    basis, eigen_values = harmonic_rows(directions)
    gram = jnp.dot(basis, basis.T, precision=lax.Precision.HIGHEST)
    chol_lower = jnp.linalg.cholesky(gram)
    partial_solve = lax.linalg.triangular_solve(chol_lower, basis, left_side=True, lower=True)
    analysis = lax.linalg.triangular_solve(
        chol_lower, partial_solve, left_side=True, lower=True, transpose_a=True
    )
    synthesis = basis.T * eigen_values[None, :]
    return (analysis, synthesis)


def advance(extended, analysis, synthesis, speeds, upwinds):
    center = extended[:, 1:-1, 1:-1, :]
    padded_x = jnp.pad(center, ((0, 0), (0, 0), (0, 0), (1, 1)))
    pairs = [
        (padded_x[:, :, :, :-2], padded_x[:, :, :, 2:]),
        (extended[:, :-2, 1:-1, :], extended[:, 2:, 1:-1, :]),
        (extended[:, 1:-1, :-2, :], extended[:, 1:-1, 2:, :]),
    ]
    transport = jnp.zeros_like(center)
    for axis_number in range(3):
        beneath, beyond = pairs[axis_number]
        rising = (upwinds[axis_number] > 0)[:, None, None, None]
        chosen = jnp.where(rising, beneath, beyond)
        transport = transport + speeds[axis_number][:, None, None, None] * (center - chosen)
    flat = center.reshape(center.shape[0], -1)
    coeffs = jnp.dot(
        analysis, flat, precision=lax.Precision.HIGHEST, preferred_element_type=jnp.float32
    )
    angular = jnp.dot(
        synthesis, coeffs, precision=lax.Precision.HIGHEST, preferred_element_type=jnp.float32
    ).reshape(center.shape)
    return center - TIME_STEP * transport + TIME_STEP * DIFFUSION * angular


def shards(fodf, directions, signs):
    analysis, synthesis = angular_maps(directions)
    speeds = jnp.abs(directions)
    field = fodf
    for sweep in range(ITERS):
        extended = padded(field, (("gz", 2), ("gy", 1)), 1)
        field = advance(extended, analysis, synthesis, speeds, signs)
    return field


def solution(mesh):
    placed = (P(None, "gy", "gz", None), P(), P())
    return jax.shard_map(
        shards, mesh=mesh, in_specs=placed, out_specs=P(None, "gy", "gz", None), check_vma=False
    )
```

profile of v0, /device:TPU:160, one launch (start us, length us, event | category | flops | bytes accessed | tf_op | source)
XLA Modules:
  0.0 172.3 jit_solution(7797901516059790657)
XLA Ops:
  0.0 1.5 copy.35
  1.5 1.3 fusion.93
  2.8 7.5 %collective-permute-start.2 = (f32[192,8,1,128]{3,1,2,0:T(8,128)}, f32[192,8,1,128]{3,1,2,0:T(8,128)}, u32[]{:S(2)}, u32[]{:S(2)}) collective-permute-start(f32[192,8,1,128]{3,1,2,0:T(8,128)} %get-tuple-element.52), channel_id=1, source_target_pairs={{8,0},{16,8},{24,16},{32,24},{40,32},{48,40},{56,48},{64,56},{72,6... | collective-permute-start | bytes 2359304 | tf_op jit(solution)/shard_map/ppermute | solution.py:25
  10.3 1.9 %collective-permute-start.1 = (f32[192,8,1,128]{3,1,2,0:T(8,128)}, f32[192,8,1,128]{3,1,2,0:T(8,128)}, u32[]{:S(2)}, u32[]{:S(2)}) collective-permute-start(f32[192,8,1,128]{3,1,2,0:T(8,128)} %get-tuple-element.51), channel_id=1, source_target_pairs={{0,8},{8,16},{16,24},{24,32},{32,40},{40,48},{48,56},{56,64},{64,7... | collective-permute-start | bytes 2359304 | tf_op jit(solution)/shard_map/ppermute | solution.py:24
  12.3 0.9 fusion.92
  13.2 1.9 %collective-permute-start.3 = (f32[192,1,2,128]{3,1,2,0:T(1,128)}, f32[192,1,2,128]{3,1,2,0:T(1,128)}, u32[]{:S(2)}, u32[]{:S(2)}) collective-permute-start(f32[192,1,2,128]{3,1,2,0:T(1,128)} %get-tuple-element.50), channel_id=1, source_target_pairs={{1,0},{2,1},{3,2},{4,3},{5,4},{6,5},{7,6},{9,8},{10,9},{11,10},{12... | collective-permute-start | bytes 589832 | tf_op jit(solution)/shard_map/ppermute | solution.py:25
  15.1 2.4 %collective-permute-start = (f32[192,1,2,128]{3,1,2,0:T(1,128)S(1)}, f32[192,1,2,128]{3,1,2,0:T(1,128)}, u32[]{:S(2)}, u32[]{:S(2)}) collective-permute-start(f32[192,1,2,128]{3,1,2,0:T(1,128)S(1)} %get-tuple-element.49), channel_id=1, source_target_pairs={{0,1},{1,2},{2,3},{3,4},{4,5},{5,6},{6,7},{8,9},{9,10},{10,11},{11... | collective-permute-start | bytes 589832 | tf_op jit(solution)/shard_map/ppermute | solution.py:24
  17.6 2.4 %reshape.60 = f32[192,2048]{1,0:T(8,128)} reshape(f32[192,8,2,128]{3,2,1,0:T(2,128)S(1)} %copy-done) | data formatting | bytes 3145728 | tf_op jit(solution)/shard_map/reshape | solution.py:102
  20.1 0.6 broadcast_multiply_fusion.3
  21.3 0.6 fusion.95
  21.9 3.5 %stack.5 = f32[45,192]{1,0:T(8,128)S(1)} concatenate(f32[1,192]{1,0:T(1,128)S(1)} %stack.4, f32[1,192]{1,0:T(1,128)S(1)} %get-tuple-element.76, f32[1,192]{1,0:T(1,128)S(1)} %get-tuple-element.102, f32[1,192]{1,0:T(1,128)S(1)} %get-tuple-element.103, f32[1,192]{1,0:T(1,128)} %get-tuple-element.118, f32[1,192]{1,0:T(1,128)S(1)} %get-tuple-element.105, ...), dimensions={0} | concatenate | bytes 69120 | tf_op jit(solution)/shard_map/stack | solution.py:73
  25.7 4.1 %cholesky.16 = f32[45,45]{1,0:T(8,128)S(1)} custom-call(f32[45,45]{1,0:T(8,128)S(1)} %fusion.71), custom_call_target="Cholesky" | custom-call | tf_op jit(solution)/shard_map/jit(cholesky)/cholesky | solution.py:79
  29.8 0.7 compare_reduce_fusion.3
  30.5 0.6 fusion.66
  31.1 3.4 %custom-call.8 = f32[1,45,45]{1,2,0:T(8,128)S(1)} custom-call(f32[1,45,45]{2,1,0:T(8,128)S(1)} %fusion.66), custom_call_target="InvertDiagBlocksLowerTriangular" | custom-call | tf_op jit(solution)/shard_map/triangular_solve | solution.py:81
  35.0 2.5 %fusion.98 = f32[45,2048]{1,0:T(8,128)S(1)} fusion(f32[45,192]{1,0:T(8,128)S(1)} %fusion.67, f32[192,2048]{1,0:T(8,128)} %reshape.60), kind=kOutput, calls=%fused_computation.226 | convolution fusion | flops 212336640 | bytes 1976064 | tf_op jit(solution)/shard_map/dot_general | solution.py:103
  37.5 2.6 %convolution_multiply_fusion.3 = f32[192,2048]{1,0:T(8,128)} fusion(f32[45,2048]{1,0:T(8,128)S(1)} %fusion.98, f32[45,192]{1,0:T(8,128)S(1)} %stack.5, f32[45]{0:T(128)S(1)} %copy-done.3), kind=kOutput, calls=%fused_computation.11 | convolution fusion | flops 212738496 | bytes 1976244 | tf_op jit(solution)/shard_map/dot_general | solution.py:106
  40.2 3.4 %mul.1542 = f32[192,8,2,128]{3,2,1,0:T(2,128)} reshape(f32[192,2048]{1,0:T(8,128)} %convolution_multiply_fusion.3) | data formatting | bytes 3145728 | tf_op jit(solution)/shard_map/mul | solution.py:109
  43.6 1.2 constant_dynamic-update-slice_fusion.2
  45.1 1.3 constant_dynamic-update-slice_fusion
  46.8 4.9 %fusion.7 = f32[192,8,2,128]{3,1,2,0:T(8,128)S(1)} fusion(f32[192,8,2,128]{3,1,2,0:T(8,128)S(1)} %copy.35, f32[192,8,1,128]{3,1,2,0:T(8,128)} %collective-permute-done.2, f32[192,8,1,128]{3,1,2,0:T(8,128)} %collective-permute-done.1, f32[192,8,4,128]{3,1,2,0:T(8,128)S(1)} %constant_dynamic-update-slice_fusion, f32[192,1,2,128]{3,1,2,0:T(1,128)} %collective-permute-done.3, ...), kind=kLoop, calls=%fused_computation.19 | loop fusion | flops 9437184 | bytes 9833280 | tf_op jit(solution)/shard_map/add | solution.py:109
  51.7 1.3 fusion.91
  53.0 0.8 copy.38
  53.8 8.1 %collective-permute-start.6 = (f32[192,8,1,128]{3,1,2,0:T(8,128)}, f32[192,8,1,128]{3,1,2,0:T(8,128)}, u32[]{:S(2)}, u32[]{:S(2)}) collective-permute-start(f32[192,8,1,128]{3,1,2,0:T(8,128)} %get-tuple-element.48), channel_id=1, source_target_pairs={{8,0},{16,8},{24,16},{32,24},{40,32},{48,40},{56,48},{64,56},{72,6... | collective-permute-start | bytes 2359304 | tf_op jit(solution)/shard_map/ppermute | solution.py:25
  61.9 1.9 %collective-permute-start.5 = (f32[192,8,1,128]{3,1,2,0:T(8,128)}, f32[192,8,1,128]{3,1,2,0:T(8,128)}, u32[]{:S(2)}, u32[]{:S(2)}) collective-permute-start(f32[192,8,1,128]{3,1,2,0:T(8,128)} %get-tuple-element.47), channel_id=1, source_target_pairs={{0,8},{8,16},{16,24},{24,32},{32,40},{40,48},{48,56},{56,64},{64,7... | collective-permute-start | bytes 2359304 | tf_op jit(solution)/shard_map/ppermute | solution.py:24
  63.9 1.0 fusion.90
  64.9 5.0 %collective-permute-start.7 = (f32[192,1,2,128]{3,1,2,0:T(1,128)}, f32[192,1,2,128]{3,1,2,0:T(1,128)S(1)}, u32[]{:S(2)}, u32[]{:S(2)}) collective-permute-start(f32[192,1,2,128]{3,1,2,0:T(1,128)} %get-tuple-element.46), channel_id=1, source_target_pairs={{1,0},{2,1},{3,2},{4,3},{5,4},{6,5},{7,6},{9,8},{10,9},{11,10},{12... | collective-permute-start | bytes 589832 | tf_op jit(solution)/shard_map/ppermute | solution.py:25
  69.8 2.1 %collective-permute-start.4 = (f32[192,1,2,128]{3,1,2,0:T(1,128)}, f32[192,1,2,128]{3,1,2,0:T(1,128)}, u32[]{:S(2)}, u32[]{:S(2)}) collective-permute-start(f32[192,1,2,128]{3,1,2,0:T(1,128)} %get-tuple-element.45), channel_id=1, source_target_pairs={{0,1},{1,2},{2,3},{3,4},{4,5},{5,6},{6,7},{8,9},{9,10},{10,11},{11... | collective-permute-start | bytes 589832 | tf_op jit(solution)/shard_map/ppermute | solution.py:24
  71.9 2.4 %reshape.61 = f32[192,2048]{1,0:T(8,128)} reshape(f32[192,8,2,128]{3,2,1,0:T(2,128)S(1)} %copy.38) | data formatting | bytes 3145728 | tf_op jit(solution)/shard_map/reshape | solution.py:102
  74.3 2.5 %fusion.99 = f32[45,2048]{1,0:T(8,128)S(1)} fusion(f32[45,192]{1,0:T(8,128)S(1)} %fusion.67, f32[192,2048]{1,0:T(8,128)} %reshape.61), kind=kOutput, calls=%fused_computation.227 | convolution fusion | flops 212336640 | bytes 1976064 | tf_op jit(solution)/shard_map/dot_general | solution.py:103
  76.8 1.5 convolution_multiply_fusion.2
  78.3 2.5 %mul.1548 = f32[192,8,2,128]{3,2,1,0:T(2,128)} reshape(f32[192,2048]{1,0:T(8,128)S(1)} %convolution_multiply_fusion.2) | data formatting | bytes 3145728 | tf_op jit(solution)/shard_map/mul | solution.py:109
  80.8 3.6 %collective-permute-done.7 = f32[192,1,2,128]{3,1,2,0:T(1,128)S(1)} collective-permute-done((f32[192,1,2,128]{3,1,2,0:T(1,128)}, f32[192,1,2,128]{3,1,2,0:T(1,128)S(1)}, u32[]{:S(2)}, u32[]{:S(2)}) %collective-permute-start.7) | collective-permute-done | bytes 196640 | tf_op jit(solution)/shard_map/ppermute | solution.py:25
  84.4 6.3 %collective-permute-done.5 = f32[192,8,1,128]{3,1,2,0:T(8,128)} collective-permute-done((f32[192,8,1,128]{3,1,2,0:T(8,128)}, f32[192,8,1,128]{3,1,2,0:T(8,128)}, u32[]{:S(2)}, u32[]{:S(2)}) %collective-permute-start.5) | collective-permute-done | bytes 786464 | tf_op jit(solution)/shard_map/ppermute | solution.py:24
  90.7 5.2 %fusion.15 = f32[192,8,2,128]{3,1,2,0:T(8,128)S(1)} fusion(f32[192,8,2,128]{3,1,2,0:T(8,128)S(1)} %fusion.7, f32[192,8,1,128]{3,1,2,0:T(8,128)} %collective-permute-done.6, f32[192,8,1,128]{3,1,2,0:T(8,128)} %collective-permute-done.5, f32[192,1,2,128]{3,1,2,0:T(1,128)S(1)} %collective-permute-done.7, f32[192,1,2,128]{3,1,2,0:T(1,128)} %collective-permute-done.4, ...), kind=kLoop, calls=%fused_computation.27 | loop fusion | flops 11010048 | bytes 6687552 | tf_op jit(solution)/shard_map/add | solution.py:109
  96.0 1.3 fusion.89
  97.2 0.8 copy.40
  98.1 3.8 %collective-permute-start.10 = (f32[192,8,1,128]{3,1,2,0:T(8,128)}, f32[192,8,1,128]{3,1,2,0:T(8,128)}, u32[]{:S(2)}, u32[]{:S(2)}) collective-permute-start(f32[192,8,1,128]{3,1,2,0:T(8,128)} %get-tuple-element.44), channel_id=1, source_target_pairs={{8,0},{16,8},{24,16},{32,24},{40,32},{48,40},{56,48},{64,56},{72,6... | collective-permute-start | bytes 2359304 | tf_op jit(solution)/shard_map/ppermute | solution.py:25
  101.9 2.0 %collective-permute-start.9 = (f32[192,8,1,128]{3,1,2,0:T(8,128)}, f32[192,8,1,128]{3,1,2,0:T(8,128)}, u32[]{:S(2)}, u32[]{:S(2)}) collective-permute-start(f32[192,8,1,128]{3,1,2,0:T(8,128)} %get-tuple-element.43), channel_id=1, source_target_pairs={{0,8},{8,16},{16,24},{24,32},{32,40},{40,48},{48,56},{56,64},{64,7... | collective-permute-start | bytes 2359304 | tf_op jit(solution)/shard_map/ppermute | solution.py:24
  103.9 1.0 fusion.88
  104.9 1.9 %collective-permute-start.11 = (f32[192,1,2,128]{3,1,2,0:T(1,128)}, f32[192,1,2,128]{3,1,2,0:T(1,128)S(1)}, u32[]{:S(2)}, u32[]{:S(2)}) collective-permute-start(f32[192,1,2,128]{3,1,2,0:T(1,128)} %get-tuple-element.42), channel_id=1, source_target_pairs={{1,0},{2,1},{3,2},{4,3},{5,4},{6,5},{7,6},{9,8},{10,9},{11,10},{12... | collective-permute-start | bytes 589832 | tf_op jit(solution)/shard_map/ppermute | solution.py:25
  106.8 2.6 %collective-permute-start.8 = (f32[192,1,2,128]{3,1,2,0:T(1,128)}, f32[192,1,2,128]{3,1,2,0:T(1,128)}, u32[]{:S(2)}, u32[]{:S(2)}) collective-permute-start(f32[192,1,2,128]{3,1,2,0:T(1,128)} %get-tuple-element.41), channel_id=1, source_target_pairs={{0,1},{1,2},{2,3},{3,4},{4,5},{5,6},{6,7},{8,9},{9,10},{10,11},{11... | collective-permute-start | bytes 589832 | tf_op jit(solution)/shard_map/ppermute | solution.py:24
  109.5 2.4 %reshape.62 = f32[192,2048]{1,0:T(8,128)} reshape(f32[192,8,2,128]{3,2,1,0:T(2,128)S(1)} %copy.40) | data formatting | bytes 3145728 | tf_op jit(solution)/shard_map/reshape | solution.py:102
  111.9 2.5 %fusion.100 = f32[45,2048]{1,0:T(8,128)S(1)} fusion(f32[45,192]{1,0:T(8,128)S(1)} %fusion.67, f32[192,2048]{1,0:T(8,128)} %reshape.62), kind=kOutput, calls=%fused_computation.228 | convolution fusion | flops 212336640 | bytes 1976064 | tf_op jit(solution)/shard_map/dot_general | solution.py:103
  114.3 1.5 convolution_multiply_fusion.1
  115.9 2.5 %mul.1554 = f32[192,8,2,128]{3,2,1,0:T(2,128)} reshape(f32[192,2048]{1,0:T(8,128)S(1)} %convolution_multiply_fusion.1) | data formatting | bytes 3145728 | tf_op jit(solution)/shard_map/mul | solution.py:109
  118.3 2.9 %collective-permute-done.11 = f32[192,1,2,128]{3,1,2,0:T(1,128)S(1)} collective-permute-done((f32[192,1,2,128]{3,1,2,0:T(1,128)}, f32[192,1,2,128]{3,1,2,0:T(1,128)S(1)}, u32[]{:S(2)}, u32[]{:S(2)}) %collective-permute-start.11) | collective-permute-done | bytes 196640 | tf_op jit(solution)/shard_map/ppermute | solution.py:25
  121.3 7.5 %collective-permute-done.9 = f32[192,8,1,128]{3,1,2,0:T(8,128)} collective-permute-done((f32[192,8,1,128]{3,1,2,0:T(8,128)}, f32[192,8,1,128]{3,1,2,0:T(8,128)}, u32[]{:S(2)}, u32[]{:S(2)}) %collective-permute-start.9) | collective-permute-done | bytes 786464 | tf_op jit(solution)/shard_map/ppermute | solution.py:24
  128.8 5.2 %fusion.23 = f32[192,8,2,128]{3,1,2,0:T(8,128)S(1)} fusion(f32[192,8,2,128]{3,1,2,0:T(8,128)S(1)} %fusion.15, f32[192,8,1,128]{3,1,2,0:T(8,128)} %collective-permute-done.10, f32[192,8,1,128]{3,1,2,0:T(8,128)} %collective-permute-done.9, f32[192,1,2,128]{3,1,2,0:T(1,128)S(1)} %collective-permute-done.11, f32[192,1,2,128]{3,1,2,0:T(1,128)} %collective-permute-done.8, ...), kind=kLoop, calls=%fused_computation.35 | loop fusion | flops 11010048 | bytes 6687552 | tf_op jit(solution)/shard_map/add | solution.py:109
  134.0 1.3 fusion.87
  135.3 0.8 copy.42
  136.1 2.2 %collective-permute-start.14 = (f32[192,8,1,128]{3,1,2,0:T(8,128)}, f32[192,8,1,128]{3,1,2,0:T(8,128)}, u32[]{:S(2)}, u32[]{:S(2)}) collective-permute-start(f32[192,8,1,128]{3,1,2,0:T(8,128)} %get-tuple-element.40), channel_id=1, source_target_pairs={{8,0},{16,8},{24,16},{32,24},{40,32},{48,40},{56,48},{64,56},{72,6... | collective-permute-start | bytes 2359304 | tf_op jit(solution)/shard_map/ppermute | solution.py:25
  138.3 3.6 %collective-permute-start.13 = (f32[192,8,1,128]{3,1,2,0:T(8,128)}, f32[192,8,1,128]{3,1,2,0:T(8,128)}, u32[]{:S(2)}, u32[]{:S(2)}) collective-permute-start(f32[192,8,1,128]{3,1,2,0:T(8,128)} %get-tuple-element.39), channel_id=1, source_target_pairs={{0,8},{8,16},{16,24},{24,32},{32,40},{40,48},{48,56},{56,64},{64,7... | collective-permute-start | bytes 2359304 | tf_op jit(solution)/shard_map/ppermute | solution.py:24
  142.0 1.0 fusion.86
  143.0 1.9 %collective-permute-start.15 = (f32[192,1,2,128]{3,1,2,0:T(1,128)}, f32[192,1,2,128]{3,1,2,0:T(1,128)S(1)}, u32[]{:S(2)}, u32[]{:S(2)}) collective-permute-start(f32[192,1,2,128]{3,1,2,0:T(1,128)} %get-tuple-element.38), channel_id=1, source_target_pairs={{1,0},{2,1},{3,2},{4,3},{5,4},{6,5},{7,6},{9,8},{10,9},{11,10},{12... | collective-permute-start | bytes 589832 | tf_op jit(solution)/shard_map/ppermute | solution.py:25
  144.9 2.7 %collective-permute-start.12 = (f32[192,1,2,128]{3,1,2,0:T(1,128)}, f32[192,1,2,128]{3,1,2,0:T(1,128)}, u32[]{:S(2)}, u32[]{:S(2)}) collective-permute-start(f32[192,1,2,128]{3,1,2,0:T(1,128)} %get-tuple-element.37), channel_id=1, source_target_pairs={{0,1},{1,2},{2,3},{3,4},{4,5},{5,6},{6,7},{8,9},{9,10},{10,11},{11... | collective-permute-start | bytes 589832 | tf_op jit(solution)/shard_map/ppermute | solution.py:24
  147.6 2.4 %reshape.63 = f32[192,2048]{1,0:T(8,128)} reshape(f32[192,8,2,128]{3,2,1,0:T(2,128)S(1)} %copy.42) | data formatting | bytes 3145728 | tf_op jit(solution)/shard_map/reshape | solution.py:102
  150.0 2.5 %fusion.101 = f32[45,2048]{1,0:T(8,128)S(1)} fusion(f32[45,192]{1,0:T(8,128)S(1)} %fusion.67, f32[192,2048]{1,0:T(8,128)} %reshape.63), kind=kOutput, calls=%fused_computation.229 | convolution fusion | flops 212336640 | bytes 1976064 | tf_op jit(solution)/shard_map/dot_general | solution.py:103
  152.4 1.5 convolution_multiply_fusion
  153.9 2.5 %mul.1560 = f32[192,8,2,128]{3,2,1,0:T(2,128)} reshape(f32[192,2048]{1,0:T(8,128)S(1)} %convolution_multiply_fusion) | data formatting | bytes 3145728 | tf_op jit(solution)/shard_map/mul | solution.py:109
  156.4 1.5 collective-permute-done.15
  157.9 7.2 %collective-permute-done.13 = f32[192,8,1,128]{3,1,2,0:T(8,128)} collective-permute-done((f32[192,8,1,128]{3,1,2,0:T(8,128)}, f32[192,8,1,128]{3,1,2,0:T(8,128)}, u32[]{:S(2)}, u32[]{:S(2)}) %collective-permute-start.13) | collective-permute-done | bytes 786464 | tf_op jit(solution)/shard_map/ppermute | solution.py:24
  165.2 5.2 %fusion.31 = f32[192,8,2,128]{3,1,2,0:T(8,128)S(1)} fusion(f32[192,8,2,128]{3,1,2,0:T(8,128)S(1)} %fusion.23, f32[192,8,1,128]{3,1,2,0:T(8,128)} %collective-permute-done.14, f32[192,8,1,128]{3,1,2,0:T(8,128)} %collective-permute-done.13, f32[192,1,2,128]{3,1,2,0:T(1,128)S(1)} %collective-permute-done.15, f32[192,1,2,128]{3,1,2,0:T(1,128)} %collective-permute-done.12, ...), kind=kLoop, calls=%fused_computation.43 | loop fusion | flops 11010048 | bytes 6687552 | tf_op jit(solution)/shard_map/add | solution.py:109
  170.4 2.0 %copy.44 = f32[192,8,2,128]{3,2,1,0:T(2,128)} copy(f32[192,8,2,128]{3,1,2,0:T(8,128)S(1)} %fusion.31) | data formatting | bytes 3145728 | tf_op jit(solution)/shard_map/add | solution.py:109
  (37 shorter events, 2.0 us)
Async XLA Ops:
  1.5 16.0 %copy-start = (f32[192,8,2,128]{3,2,1,0:T(2,128)S(1)}, f32[192,8,2,128]{3,2,1,0:T(2,128)}, u32[]{:S(2)}) copy-start(f32[192,8,2,128]{3,2,1,0:T(2,128)} %param.4) | copy-start | bytes 4718596
  2.8 42.3 %collective-permute-start.2 = (f32[192,8,1,128]{3,1,2,0:T(8,128)}, f32[192,8,1,128]{3,1,2,0:T(8,128)}, u32[]{:S(2)}, u32[]{:S(2)}) collective-permute-start(f32[192,8,1,128]{3,1,2,0:T(8,128)} %get-tuple-element.52), channel_id=1, source_target_pairs={{8,0},{16,8},{24,16},{32,24},{40,32},{48,40},{56,48},{64,56},{72,6... | collective-permute-start | bytes 2359304 | tf_op jit(solution)/shard_map/ppermute | solution.py:25
  10.3 33.3 %collective-permute-start.1 = (f32[192,8,1,128]{3,1,2,0:T(8,128)}, f32[192,8,1,128]{3,1,2,0:T(8,128)}, u32[]{:S(2)}, u32[]{:S(2)}) collective-permute-start(f32[192,8,1,128]{3,1,2,0:T(8,128)} %get-tuple-element.51), channel_id=1, source_target_pairs={{0,8},{8,16},{16,24},{24,32},{32,40},{40,48},{48,56},{56,64},{64,7... | collective-permute-start | bytes 2359304 | tf_op jit(solution)/shard_map/ppermute | solution.py:24
  13.2 33.3 %collective-permute-start.3 = (f32[192,1,2,128]{3,1,2,0:T(1,128)}, f32[192,1,2,128]{3,1,2,0:T(1,128)}, u32[]{:S(2)}, u32[]{:S(2)}) collective-permute-start(f32[192,1,2,128]{3,1,2,0:T(1,128)} %get-tuple-element.50), channel_id=1, source_target_pairs={{1,0},{2,1},{3,2},{4,3},{5,4},{6,5},{7,6},{9,8},{10,9},{11,10},{12... | collective-permute-start | bytes 589832 | tf_op jit(solution)/shard_map/ppermute | solution.py:25
  15.1 4.8 %copy-start.2 = (f32[3,192]{1,0:T(4,128)S(1)}, f32[3,192]{1,0:T(4,128)}, u32[]{:S(2)}) copy-start(f32[3,192]{1,0:T(4,128)} %param.5) | copy-start | bytes 6916
  15.1 31.4 %collective-permute-start = (f32[192,1,2,128]{3,1,2,0:T(1,128)S(1)}, f32[192,1,2,128]{3,1,2,0:T(1,128)}, u32[]{:S(2)}, u32[]{:S(2)}) collective-permute-start(f32[192,1,2,128]{3,1,2,0:T(1,128)S(1)} %get-tuple-element.49), channel_id=1, source_target_pairs={{0,1},{1,2},{2,3},{3,4},{4,5},{5,6},{6,7},{8,9},{9,10},{10,11},{11... | collective-permute-start | bytes 589832 | tf_op jit(solution)/shard_map/ppermute | solution.py:24
  20.0 17.5 %copy-start.3 = (f32[45]{0:T(128)S(1)}, f32[45]{0:T(128)}, u32[]{:S(2)}) copy-start(f32[45]{0:T(128)} %constant.246.clone) | copy-start | bytes 544
  40.2 3.4 %copy-start.4 = (s32[3,192]{1,0:T(4,128)S(1)}, s32[3,192]{1,0:T(4,128)}, u32[]{:S(2)}) copy-start(s32[3,192]{1,0:T(4,128)} %param.6) | copy-start | bytes 6916
  45.1 1.7 copy-start.1
  53.8 30.6 %collective-permute-start.6 = (f32[192,8,1,128]{3,1,2,0:T(8,128)}, f32[192,8,1,128]{3,1,2,0:T(8,128)}, u32[]{:S(2)}, u32[]{:S(2)}) collective-permute-start(f32[192,8,1,128]{3,1,2,0:T(8,128)} %get-tuple-element.48), channel_id=1, source_target_pairs={{8,0},{16,8},{24,16},{32,24},{40,32},{48,40},{56,48},{64,56},{72,6... | collective-permute-start | bytes 2359304 | tf_op jit(solution)/shard_map/ppermute | solution.py:25
  61.9 28.8 %collective-permute-start.5 = (f32[192,8,1,128]{3,1,2,0:T(8,128)}, f32[192,8,1,128]{3,1,2,0:T(8,128)}, u32[]{:S(2)}, u32[]{:S(2)}) collective-permute-start(f32[192,8,1,128]{3,1,2,0:T(8,128)} %get-tuple-element.47), channel_id=1, source_target_pairs={{0,8},{8,16},{16,24},{24,32},{32,40},{40,48},{48,56},{56,64},{64,7... | collective-permute-start | bytes 2359304 | tf_op jit(solution)/shard_map/ppermute | solution.py:24
  64.9 19.5 %collective-permute-start.7 = (f32[192,1,2,128]{3,1,2,0:T(1,128)}, f32[192,1,2,128]{3,1,2,0:T(1,128)S(1)}, u32[]{:S(2)}, u32[]{:S(2)}) collective-permute-start(f32[192,1,2,128]{3,1,2,0:T(1,128)} %get-tuple-element.46), channel_id=1, source_target_pairs={{1,0},{2,1},{3,2},{4,3},{5,4},{6,5},{7,6},{9,8},{10,9},{11,10},{12... | collective-permute-start | bytes 589832 | tf_op jit(solution)/shard_map/ppermute | solution.py:25
  69.8 14.5 %collective-permute-start.4 = (f32[192,1,2,128]{3,1,2,0:T(1,128)}, f32[192,1,2,128]{3,1,2,0:T(1,128)}, u32[]{:S(2)}, u32[]{:S(2)}) collective-permute-start(f32[192,1,2,128]{3,1,2,0:T(1,128)} %get-tuple-element.45), channel_id=1, source_target_pairs={{0,1},{1,2},{2,3},{3,4},{4,5},{5,6},{6,7},{8,9},{9,10},{10,11},{11... | collective-permute-start | bytes 589832 | tf_op jit(solution)/shard_map/ppermute | solution.py:24
  98.1 23.2 %collective-permute-start.10 = (f32[192,8,1,128]{3,1,2,0:T(8,128)}, f32[192,8,1,128]{3,1,2,0:T(8,128)}, u32[]{:S(2)}, u32[]{:S(2)}) collective-permute-start(f32[192,8,1,128]{3,1,2,0:T(8,128)} %get-tuple-element.44), channel_id=1, source_target_pairs={{8,0},{16,8},{24,16},{32,24},{40,32},{48,40},{56,48},{64,56},{72,6... | collective-permute-start | bytes 2359304 | tf_op jit(solution)/shard_map/ppermute | solution.py:25
  101.9 26.9 %collective-permute-start.9 = (f32[192,8,1,128]{3,1,2,0:T(8,128)}, f32[192,8,1,128]{3,1,2,0:T(8,128)}, u32[]{:S(2)}, u32[]{:S(2)}) collective-permute-start(f32[192,8,1,128]{3,1,2,0:T(8,128)} %get-tuple-element.43), channel_id=1, source_target_pairs={{0,8},{8,16},{16,24},{24,32},{32,40},{40,48},{48,56},{56,64},{64,7... | collective-permute-start | bytes 2359304 | tf_op jit(solution)/shard_map/ppermute | solution.py:24
  104.9 16.4 %collective-permute-start.11 = (f32[192,1,2,128]{3,1,2,0:T(1,128)}, f32[192,1,2,128]{3,1,2,0:T(1,128)S(1)}, u32[]{:S(2)}, u32[]{:S(2)}) collective-permute-start(f32[192,1,2,128]{3,1,2,0:T(1,128)} %get-tuple-element.42), channel_id=1, source_target_pairs={{1,0},{2,1},{3,2},{4,3},{5,4},{6,5},{7,6},{9,8},{10,9},{11,10},{12... | collective-permute-start | bytes 589832 | tf_op jit(solution)/shard_map/ppermute | solution.py:25
  106.8 14.5 %collective-permute-start.8 = (f32[192,1,2,128]{3,1,2,0:T(1,128)}, f32[192,1,2,128]{3,1,2,0:T(1,128)}, u32[]{:S(2)}, u32[]{:S(2)}) collective-permute-start(f32[192,1,2,128]{3,1,2,0:T(1,128)} %get-tuple-element.41), channel_id=1, source_target_pairs={{0,1},{1,2},{2,3},{3,4},{4,5},{5,6},{6,7},{8,9},{9,10},{10,11},{11... | collective-permute-start | bytes 589832 | tf_op jit(solution)/shard_map/ppermute | solution.py:24
  136.1 21.8 %collective-permute-start.14 = (f32[192,8,1,128]{3,1,2,0:T(8,128)}, f32[192,8,1,128]{3,1,2,0:T(8,128)}, u32[]{:S(2)}, u32[]{:S(2)}) collective-permute-start(f32[192,8,1,128]{3,1,2,0:T(8,128)} %get-tuple-element.40), channel_id=1, source_target_pairs={{8,0},{16,8},{24,16},{32,24},{40,32},{48,40},{56,48},{64,56},{72,6... | collective-permute-start | bytes 2359304 | tf_op jit(solution)/shard_map/ppermute | solution.py:25
  138.3 26.8 %collective-permute-start.13 = (f32[192,8,1,128]{3,1,2,0:T(8,128)}, f32[192,8,1,128]{3,1,2,0:T(8,128)}, u32[]{:S(2)}, u32[]{:S(2)}) collective-permute-start(f32[192,8,1,128]{3,1,2,0:T(8,128)} %get-tuple-element.39), channel_id=1, source_target_pairs={{0,8},{8,16},{16,24},{24,32},{32,40},{40,48},{48,56},{56,64},{64,7... | collective-permute-start | bytes 2359304 | tf_op jit(solution)/shard_map/ppermute | solution.py:24
  143.0 14.9 %collective-permute-start.15 = (f32[192,1,2,128]{3,1,2,0:T(1,128)}, f32[192,1,2,128]{3,1,2,0:T(1,128)S(1)}, u32[]{:S(2)}, u32[]{:S(2)}) collective-permute-start(f32[192,1,2,128]{3,1,2,0:T(1,128)} %get-tuple-element.38), channel_id=1, source_target_pairs={{1,0},{2,1},{3,2},{4,3},{5,4},{6,5},{7,6},{9,8},{10,9},{11,10},{12... | collective-permute-start | bytes 589832 | tf_op jit(solution)/shard_map/ppermute | solution.py:25
  144.9 13.0 %collective-permute-start.12 = (f32[192,1,2,128]{3,1,2,0:T(1,128)}, f32[192,1,2,128]{3,1,2,0:T(1,128)}, u32[]{:S(2)}, u32[]{:S(2)}) collective-permute-start(f32[192,1,2,128]{3,1,2,0:T(1,128)} %get-tuple-element.37), channel_id=1, source_target_pairs={{0,1},{1,2},{2,3},{3,4},{4,5},{5,6},{6,7},{8,9},{9,10},{10,11},{11... | collective-permute-start | bytes 589832 | tf_op jit(solution)/shard_map/ppermute | solution.py:24
where the time goes:
time: 174 us; the launch traced here: 172 us
  starting transfers between devices  51.7 us (30%)
  local copies, waits for them, and re-layouts  42 us (24%)
  other arithmetic  31.4 us (18%)
  waiting for transfers between devices  29.1 us (17%)
  matrix products  17.6 us (10%)
    ppermute x8, starting transfers between devices, padded(): lax.ppermute(initial, axis, [(b, a) for a, b in up])  32.4 us
    ppermute x8, waiting for transfers between devices, padded(): lax.ppermute(last, axis, up)  21.1 us
    add x4, other arithmetic, advance(): return center - TIME_STEP * transport + TIME_STEP * DIFFUSION * angular  20.6 us
    ppermute x8, starting transfers between devices, padded(): lax.ppermute(last, axis, up)  19.3 us
    mul x4, local copies, waits for them, and re-layouts, advance(): return center - TIME_STEP * transport + TIME_STEP * DIFFUSION * angular  10.9 us
    dot_general x4, matrix products, advance(): jnp.dot(analysis, flat, precision=lax.Precision.HIGHEST, preferred_elemen...  9.88 us
    reshape x4, local copies, waits for them, and re-layouts, advance(): flat = center.reshape(center.shape[0], -1)  9.6 us
    slice x8, local copies, waits for them, and re-layouts, padded(): last = lax.slice_in_dim(value, length - width, length, axis=dim)  8.98 us
  transfers between devices with their start and end apart: 16, of which 6 were waited for; matrix products, arithmetic and copies ran while one was open for 34% of the time, Pallas kernels for 0%

commit v1 on v0

v1 whole, which is shorter than its diff:
```python
import math

import jax
import jax.numpy as jnp
from jax import lax
from jax.experimental import pallas as pl
from jax.experimental.pallas import tpu as pltpu
from jax.sharding import PartitionSpec as P

LMAX = 8
ITERS = 4
TIME_STEP = 0.5
DIFFUSION = 0.02

HALF = 96
LANES = 128
MODES = 45
MODES_PAD = 48
CHUNK = 16
HIGHEST = lax.Precision.HIGHEST
MESH = pl.DeviceIdType.MESH

AX, AY, AZ, CENTER, SX, SY, SZ = range(7)


def double_factorial(value):
    result = 1
    while value > 1:
        result = result * value
        value = value - 2
    return result


def harmonic_rows(along_x, along_y, along_z):
    cosines = [jnp.ones_like(along_x)]
    sines = [jnp.zeros_like(along_x)]
    for order in range(1, LMAX + 1):
        cosines.append(cosines[-1] * along_x - sines[-1] * along_y)
        sines.append(cosines[-2] * along_y + sines[-1] * along_x)
    legendre = {}
    for order in range(LMAX + 1):
        legendre[order, order] = double_factorial(2 * order - 1) * jnp.ones_like(along_z)
        if order + 1 <= LMAX:
            legendre[order + 1, order] = (2 * order + 1) * along_z * legendre[order, order]
        for degree in range(order + 2, LMAX + 1):
            legendre[degree, order] = (
                (2 * degree - 1) * along_z * legendre[degree - 1, order]
                - (degree + order - 1) * legendre[degree - 2, order]
            ) * (1.0 / (degree - order))
    rows = []
    for degree in range(0, LMAX + 1, 2):
        for order in range(degree + 1):
            norm = math.sqrt(
                (2 * degree + 1) * math.factorial(degree - order) / math.factorial(degree + order)
            )
            eigenvalue = -float(degree * (degree + 1))
            scaled = norm * legendre[degree, order]
            rows.append((scaled * cosines[order], eigenvalue))
            if order > 0:
                rows.append((scaled * sines[order], eigenvalue))
    return rows


def angular_matrix(dirs, basis, scaled, left, right):
    valid = lax.broadcasted_iota(jnp.int32, (1, LANES), 1) < HALF
    basis[...] = jnp.zeros_like(basis)
    scaled[...] = jnp.zeros_like(scaled)
    left[...] = jnp.zeros_like(left)
    right[...] = jnp.zeros_like(right)
    along = [dirs[a : a + 1, 0:LANES] for a in range(3)]
    for j, (row, eigenvalue) in enumerate(harmonic_rows(*along)):
        row = jnp.where(valid, row, 0.0)
        basis[j : j + 1, :] = row
        scaled[j : j + 1, :] = (TIME_STEP * DIFFUSION * eigenvalue) * row
    b, s = basis[...], scaled[...]
    gram = 2.0 * lax.dot_general(
        b, jnp.concatenate([b, jnp.zeros((LANES - MODES_PAD, LANES), jnp.float32)], 0),
        (((1,), (1,)), ((), ())), precision=HIGHEST, preferred_element_type=jnp.float32,
    )
    index = lax.broadcasted_iota(jnp.int32, (MODES_PAD, LANES), 0)
    for k in range(MODES):
        column = jnp.broadcast_to(gram[:, k : k + 1], (MODES_PAD, LANES))
        inverse = 1.0 / column[k : k + 1, :]
        gram_row, b_row, s_row = gram[k : k + 1, :], b[k : k + 1, :], s[k : k + 1, :]
        left[k : k + 1, :] = s_row
        right[k : k + 1, :] = b_row * inverse
        if k + 1 < MODES:
            factor = jnp.where(index > k, column, 0.0)
            gram = gram - factor * (gram_row * inverse)
            b = b - factor * (b_row * inverse)
            s = s - factor * (s_row * inverse)
    return lax.dot_general(
        left[...].T, right[...], (((1,), (0,)), ((), ())), precision=HIGHEST,
        preferred_element_type=jnp.float32,
    )


def kernel(
    fodf, dirs_hbm, signs_hbm, out,
    stage, dirs, signs, coef, basis, scaled, left, right, mat_hi, mat_lo, angular, p, q, u, v,
    in_sem, small_sem, z_send, z_recv, y_send, y_recv,
):
    ny, nz = p.shape[2], u.shape[1]
    gz, gy = lax.axis_index("gz"), lax.axis_index("gy")
    gz_last, gy_last = lax.axis_size("gz") - 1, lax.axis_size("gy") - 1
    below, above = gz > 0, gz < gz_last
    before, after = gy > 0, gy < gy_last

    def load(r):
        return pltpu.make_async_copy(fodf.at[:, r, 0, :], stage.at[r], in_sem.at[r])

    def store(r):
        return pltpu.make_async_copy(stage.at[r], out.at[:, r, 0, :], in_sem.at[r])

    def z_up(s, y):
        return pltpu.make_async_remote_copy(
            p.at[s, nz, y], p.at[s, 0, y], z_send.at[0, s, y], z_recv.at[0, s, y],
            device_id=(gz + 1, gy), device_id_type=MESH,
        )

    def z_down(s, y):
        return pltpu.make_async_remote_copy(
            q.at[s, 0, y], q.at[s, nz, y], z_send.at[1, s, y], z_recv.at[1, s, y],
            device_id=(gz - 1, gy), device_id_type=MESH,
        )

    def y_up(s):
        return pltpu.make_async_remote_copy(
            u.at[s, :, ny], u.at[s, :, 0], y_send.at[0, s], y_recv.at[0, s],
            device_id=(gz, gy + 1), device_id_type=MESH,
        )

    def y_down(s):
        return pltpu.make_async_remote_copy(
            v.at[s, :, 0], v.at[s, :, ny], y_send.at[1, s], y_recv.at[1, s],
            device_id=(gz, gy - 1), device_id_type=MESH,
        )

    def send(s, y):
        pl.when(above)(lambda: z_up(s, y).start())
        pl.when(below)(lambda: z_down(s, y).start())
        pl.when(jnp.logical_and(y == 0, before))(lambda: y_down(s).start())
        pl.when(jnp.logical_and(y == ny - 1, after))(lambda: y_up(s).start())

    def receive(s, y):
        pl.when(below)(lambda: z_up(s, y).wait_recv())
        pl.when(above)(lambda: z_down(s, y).wait_recv())
        pl.when(jnp.logical_and(y == 0, before))(lambda: y_up(s).wait_recv())
        pl.when(jnp.logical_and(y == ny - 1, after))(lambda: y_down(s).wait_recv())

    small = [
        pltpu.make_async_copy(dirs_hbm, dirs, small_sem.at[0]),
        pltpu.make_async_copy(signs_hbm, signs, small_sem.at[1]),
    ]
    for copy in small:
        copy.start()
    for r in range(ny * nz):
        load(r).start()

    barrier = pltpu.get_barrier_semaphore()
    for there, target in (
        (below, (gz - 1, gy)), (above, (gz + 1, gy)), (before, (gz, gy - 1)), (after, (gz, gy + 1)),
    ):
        @pl.when(there)
        def _():
            pl.semaphore_signal(barrier, inc=1, device_id=target, device_id_type=MESH)

    @pl.when(gz == 0)
    def _():
        p[:, 0] = jnp.zeros_like(p[:, 0])

    @pl.when(gz == gz_last)
    def _():
        q[:, nz] = jnp.zeros_like(q[:, nz])

    @pl.when(gy == 0)
    def _():
        u[:, :, 0] = jnp.zeros_like(u[:, :, 0])

    @pl.when(gy == gy_last)
    def _():
        v[:, :, ny] = jnp.zeros_like(v[:, :, ny])

    for copy in small:
        copy.wait()
    half_speed = TIME_STEP * jnp.abs(dirs[:, 0:LANES])
    sign = signs[:, 0:LANES].astype(jnp.float32)
    sign_z = sign[2:3]
    rows = [half_speed[0:1], half_speed[1:2], half_speed[2:3]]
    rows.append(1.0 - (rows[0] + rows[1] + rows[2]))
    rows += [sign[0:1] * sign_z, sign[1:2] * sign_z, sign_z]
    table = jnp.concatenate(rows + [jnp.zeros((LANES - len(rows), LANES), jnp.float32)], 0).T
    for c in range(len(rows)):
        coef[c] = jnp.broadcast_to(table[0:HALF, c : c + 1], (HALF, LANES))

    peers = sum(there.astype(jnp.int32) for there in (below, above, before, after))
    pl.semaphore_wait(barrier, peers)

    def first(y, carry):
        for z in range(nz):
            r = y * nz + z
            load(r).wait()
            for c in range(0, HALF, CHUNK):
                lines = slice(c, c + CHUNK)
                one, other = stage[r, c : c + CHUNK, :], stage[r, HALF + c : HALF + c + CHUNK, :]
                upward, along_y = coef[SZ, lines] > 0, coef[SY, lines] > 0
                up, down = jnp.where(upward, one, other), jnp.where(upward, other, one)
                p[0, z + 1, y, lines] = up
                q[0, z, y, lines] = down
                u[0, z, y + 1, lines] = jnp.where(along_y, up, down)
                v[0, z, y, lines] = jnp.where(along_y, down, up)
        send(0, y)
        return carry

    lax.fori_loop(0, ny, first, 0)

    matrix = angular_matrix(dirs, basis, scaled, left, right)[0:HALF, 0:HALF]
    high = matrix.astype(jnp.bfloat16)
    mat_hi[...] = high
    mat_lo[...] = (matrix - high.astype(jnp.float32)).astype(jnp.bfloat16)

    lane = lax.broadcasted_iota(jnp.int32, (CHUNK, LANES), 1)

    def advance(s, y, last):
        total = jnp.concatenate([p[s, z + 1, y] + q[s, z, y] for z in range(nz)], 1)
        total_hi = total.astype(jnp.bfloat16)
        total_lo = (total - total_hi.astype(jnp.float32)).astype(jnp.bfloat16)
        hi, lo = mat_hi[...], mat_lo[...]
        angular[...] = (
            jnp.dot(hi, total_hi, preferred_element_type=jnp.float32)
            + jnp.dot(hi, total_lo, preferred_element_type=jnp.float32)
            + jnp.dot(lo, total_hi, preferred_element_type=jnp.float32)
        )
        receive(s, y)
        for z in range(nz):
            for c in range(0, HALF, CHUNK):
                lines = slice(c, c + CHUNK)
                up, down = p[s, z + 1, y, lines], q[s, z, y, lines]
                along_x, along_y = coef[SX, lines] > 0, coef[SY, lines] > 0
                rising, falling = jnp.where(along_x, up, down), jnp.where(along_x, down, up)
                rising = jnp.where(lane == 0, 0.0, pltpu.roll(rising, 1, 1))
                falling = jnp.where(lane == LANES - 1, 0.0, pltpu.roll(falling, LANES - 1, 1))
                y_low, y_high = u[s, z, y, lines], v[s, z, y + 1, lines]
                ang = angular[lines, z * LANES : (z + 1) * LANES]
                ax, ay, az, center = (coef[i, lines] for i in (AX, AY, AZ, CENTER))
                new_up = (
                    center * up + ang + ax * jnp.where(along_x, rising, falling)
                    + ay * jnp.where(along_y, y_low, y_high) + az * p[s, z, y, lines]
                )
                new_down = (
                    center * down + ang + ax * jnp.where(along_x, falling, rising)
                    + ay * jnp.where(along_y, y_high, y_low) + az * q[s, z + 1, y, lines]
                )
                if last:
                    r = y * nz + z
                    upward = coef[SZ, lines] > 0
                    stage[r, c : c + CHUNK, :] = jnp.where(upward, new_up, new_down)
                    stage[r, HALF + c : HALF + c + CHUNK, :] = jnp.where(upward, new_down, new_up)
                else:
                    p[s + 1, z + 1, y, lines] = new_up
                    q[s + 1, z, y, lines] = new_down
                    u[s + 1, z, y + 1, lines] = jnp.where(along_y, new_up, new_down)
                    v[s + 1, z, y, lines] = jnp.where(along_y, new_down, new_up)

    def middle(i, carry):
        s, y = i // ny, i % ny
        advance(s, y, False)
        send(s + 1, y)
        return carry

    lax.fori_loop(0, (ITERS - 1) * ny, middle, 0)

    def final(y, carry):
        advance(ITERS - 1, y, True)
        for z in range(nz):
            store(y * nz + z).start()
        return carry

    lax.fori_loop(0, ny, final, 0)

    def sent(i, carry):
        s, y = i // ny, i % ny
        pl.when(above)(lambda: z_up(s, y).wait_send())
        pl.when(below)(lambda: z_down(s, y).wait_send())
        return carry

    lax.fori_loop(0, ITERS * ny, sent, 0)
    for s in range(ITERS):
        pl.when(after)(lambda: y_up(s).wait_send())
        pl.when(before)(lambda: y_down(s).wait_send())
    for r in range(ny * nz):
        store(r).wait()


def shards(fodf, directions, signs):
    orientations, ny, nz, _ = fodf.shape
    f32, vmem, dma = jnp.float32, pltpu.VMEM, pltpu.SemaphoreType.DMA
    rows = fodf.reshape(orientations, ny * nz, 1, LANES)
    enhanced = pl.pallas_call(
        kernel,
        out_shape=jax.ShapeDtypeStruct(rows.shape, f32),
        in_specs=[pl.BlockSpec(memory_space=pl.ANY)] * 3,
        out_specs=pl.BlockSpec(memory_space=pl.ANY),
        scratch_shapes=[
            vmem((ny * nz, orientations, LANES), f32),
            vmem((3, orientations), f32),
            vmem((3, orientations), jnp.int32),
            vmem((7, HALF, LANES), f32),
            vmem((MODES_PAD, LANES), f32),
            vmem((MODES_PAD, LANES), f32),
            vmem((MODES_PAD, LANES), f32),
            vmem((MODES_PAD, LANES), f32),
            vmem((HALF, HALF), jnp.bfloat16),
            vmem((HALF, HALF), jnp.bfloat16),
            vmem((HALF, nz * LANES), f32),
            vmem((ITERS, nz + 1, ny, HALF, LANES), f32),
            vmem((ITERS, nz + 1, ny, HALF, LANES), f32),
            vmem((ITERS, nz, ny + 1, HALF, LANES), f32),
            vmem((ITERS, nz, ny + 1, HALF, LANES), f32),
            dma((ny * nz,)),
            dma((2,)),
            dma((2, ITERS, ny)),
            dma((2, ITERS, ny)),
            dma((2, ITERS)),
            dma((2, ITERS)),
        ],
        compiler_params=pltpu.CompilerParams(
            collective_id=0, has_side_effects=True, vmem_limit_bytes=48 * 1024 * 1024
        ),
    )(rows, directions, signs)
    return enhanced.reshape(fodf.shape)


def solution(mesh):
    placed = (P(None, "gy", "gz", None), P(), P())
    return jax.shard_map(
        shards, mesh=mesh, in_specs=placed, out_specs=P(None, "gy", "gz", None), check_vma=False
    )
```

time: 174 us -> 57.8 us (0.33)
  Pallas kernels: 0 us -> 53.7 us
  starting transfers between devices: 51.7 us -> 0 us
  local copies, waits for them, and re-layouts: 42 us -> 3.93 us
  other arithmetic: 31.4 us -> 0 us
  waiting for transfers between devices: 29.1 us -> 0 us
  matrix products: 17.6 us -> 0 us
    pallas_call x0 -> x1, Pallas kernels: none -> 53.7 us  [shards(): pl.pallas_call(kernel, out_shape=jax.ShapeDtypeStruct(rows.shape, f32), i...]
    ppermute x16 -> x0, starting transfers between devices: 51.7 us -> none  [the longest x8 32.4 us: padded(): lax.ppermute(initial, axis, [(b, a) for a, b in up])]
    ppermute x16 -> x0, waiting for transfers between devices: 29.1 us -> none  [the longest x8 21.1 us: padded(): lax.ppermute(last, axis, up)]
    add x4 -> x0, other arithmetic: 20.6 us -> none  [advance(): return center - TIME_STEP * transport + TIME_STEP * DIFFUSION * angular]
    dot_general x9 -> x0, matrix products: 17.2 us -> none  [the longest x4 9.88 us: advance(): jnp.dot(analysis, flat, precision=lax.Precision.HIGHEST, preferred_elemen...]
    mul x4 -> x0, local copies, waits for them, and re-layouts: 10.9 us -> none  [advance(): return center - TIME_STEP * transport + TIME_STEP * DIFFUSION * angular]
    reshape x4 -> x0, local copies, waits for them, and re-layouts: 9.6 us -> none  [advance(): flat = center.reshape(center.shape[0], -1)]
    slice x9 -> x0, local copies, waits for them, and re-layouts: 8.98 us -> none  [the longest x8 8.98 us: padded(): last = lax.slice_in_dim(value, length - width, length, axis=dim)]
  transfers between devices with their start and end apart: 16 -> 0, of which waited for: 6 -> 0; matrix products, arithmetic and copies ran while one was open for 34% -> 0% of each run, Pallas kernels for 0% -> 0%
where the time goes in v1:
time: 57.8 us; the launch traced here: 57.7 us
  Pallas kernels  53.7 us (93%)
  local copies, waits for them, and re-layouts  3.93 us (7%)
    pallas_call x1, Pallas kernels, shards(): pl.pallas_call(kernel, out_shape=jax.ShapeDtypeStruct(rows.shape, f32), i...  53.7 us
    unnamed x7, local copies, waits for them, and re-layouts  3.93 us

profile of v1, /device:TPU:160, one launch (start us, length us, event | category | flops | bytes accessed | tf_op | source)
XLA Modules:
  0.0 57.7 jit_solution(7333753115112444777)
XLA Ops:
  0.0 0.0 copy-start
  0.0 1.4 %copy-done = f32[192,8,2,128]{3,2,1,0:T(2,128)S(1)} copy-done((f32[192,8,2,128]{3,2,1,0:T(2,128)S(1)}, f32[192,8,2,128]{3,2,1,0:T(2,128)}, u32[]{:S(2)}) %copy-start) | copy-done | bytes 1572888
  1.4 0.0 copy-start.1
  1.4 0.7 %copy-done.1 = f32[3,192]{1,0:T(4,128)S(1)} copy-done((f32[3,192]{1,0:T(4,128)S(1)}, f32[3,192]{1,0:T(4,128)}, u32[]{:S(2)}) %copy-start.1) | copy-done | bytes 2328
  2.1 0.0 copy-start.2
  2.1 0.7 %copy-done.2 = s32[3,192]{1,0:T(4,128)S(1)} copy-done((s32[3,192]{1,0:T(4,128)S(1)}, s32[3,192]{1,0:T(4,128)}, u32[]{:S(2)}) %copy-start.2) | copy-done | bytes 2328
  2.8 53.7 %shard_map.37 = f32[192,16,1,128]{3,2,1,0:T(1,128)S(1)} custom-call(f32[192,16,1,128]{3,2,1,0:T(1,128)S(1)} %bitcast.3, f32[3,192]{1,0:T(4,128)S(1)} %copy-done.1, s32[3,192]{1,0:T(4,128)S(1)} %copy-done.2), custom_call_target="tpu_custom_call" | custom-call | tf_op jit(solution)/shard_map/pallas_call | solution.py:299
  56.5 1.1 %copy.5 = f32[192,8,2,128]{3,2,1,0:T(2,128)} copy(f32[192,8,2,128]{3,2,1,0:T(2,128)S(1)} %bitcast.2) | data formatting | bytes 3145728
Async XLA Ops:
  0.0 1.4 %copy-start = (f32[192,8,2,128]{3,2,1,0:T(2,128)S(1)}, f32[192,8,2,128]{3,2,1,0:T(2,128)}, u32[]{:S(2)}) copy-start(f32[192,8,2,128]{3,2,1,0:T(2,128)} %param.3) | copy-start | bytes 4718596
  1.4 0.7 %copy-start.1 = (f32[3,192]{1,0:T(4,128)S(1)}, f32[3,192]{1,0:T(4,128)}, u32[]{:S(2)}) copy-start(f32[3,192]{1,0:T(4,128)} %dirs_hbm.1) | copy-start | bytes 6916
  2.1 0.7 %copy-start.2 = (s32[3,192]{1,0:T(4,128)S(1)}, s32[3,192]{1,0:T(4,128)}, u32[]{:S(2)}) copy-start(s32[3,192]{1,0:T(4,128)} %signs_hbm.1) | copy-start | bytes 6916

commit v2 on v1

--- a/solution.py
+++ b/solution.py
@@ -17,6 +17,7 @@
 MODES = 45
 MODES_PAD = 48
 CHUNK = 16
+RELAYED = 3
 HIGHEST = lax.Precision.HIGHEST
 MESH = pl.DeviceIdType.MESH
 
@@ -97,14 +98,18 @@
 
 def kernel(
     fodf, dirs_hbm, signs_hbm, out,
-    stage, dirs, signs, coef, basis, scaled, left, right, mat_hi, mat_lo, angular, p, q, u, v,
-    in_sem, small_sem, z_send, z_recv, y_send, y_recv,
+    stage, dirs, signs, coef, basis, scaled, left, right, mat_hi, mat_lo, angular, p, q, u, v, relay,
+    in_sem, small_sem, z_send, z_recv, y_send, y_recv, relay_recv,
 ):
     ny, nz = p.shape[2], u.shape[1]
+    kept = ny - RELAYED
     gz, gy = lax.axis_index("gz"), lax.axis_index("gy")
     gz_last, gy_last = lax.axis_size("gz") - 1, lax.axis_size("gy") - 1
     below, above = gz > 0, gz < gz_last
     before, after = gy > 0, gy < gy_last
+    seam_high = (gz_last + 1) // 2
+    seam_low = seam_high - 1
+    is_low, is_high, is_first, is_last = gz == seam_low, gz == seam_high, gz == 0, gz == gz_last
 
     def load(r):
         return pltpu.make_async_copy(fodf.at[:, r, 0, :], stage.at[r], in_sem.at[r])
@@ -124,6 +129,30 @@
             device_id=(gz - 1, gy), device_id_type=MESH,
         )
 
+    def relay_up(s, y):
+        return pltpu.make_async_remote_copy(
+            p.at[s, nz, y], relay.at[s, y - kept], z_send.at[0, s, y], relay_recv.at[s, y - kept],
+            device_id=(gz_last, gy), device_id_type=MESH,
+        )
+
+    def relay_down(s, y):
+        return pltpu.make_async_remote_copy(
+            q.at[s, 0, y], relay.at[s, y - kept], z_send.at[1, s, y], relay_recv.at[s, y - kept],
+            device_id=(0, gy), device_id_type=MESH,
+        )
+
+    def forward_up(s, y):
+        return pltpu.make_async_remote_copy(
+            relay.at[s, y - kept], p.at[s, 0, y], z_send.at[0, s, y], z_recv.at[0, s, y],
+            device_id=(seam_high, gy), device_id_type=MESH,
+        )
+
+    def forward_down(s, y):
+        return pltpu.make_async_remote_copy(
+            relay.at[s, y - kept], q.at[s, nz, y], z_send.at[1, s, y], z_recv.at[1, s, y],
+            device_id=(seam_low, gy), device_id_type=MESH,
+        )
+
     def y_up(s):
         return pltpu.make_async_remote_copy(
             u.at[s, :, ny], u.at[s, :, 0], y_send.at[0, s], y_recv.at[0, s],
@@ -137,8 +166,12 @@
         )
 
     def send(s, y):
-        pl.when(above)(lambda: z_up(s, y).start())
-        pl.when(below)(lambda: z_down(s, y).start())
+        far = y >= kept
+        round_up, round_down = jnp.logical_and(is_low, far), jnp.logical_and(is_high, far)
+        pl.when(jnp.logical_and(above, jnp.logical_not(round_up)))(lambda: z_up(s, y).start())
+        pl.when(jnp.logical_and(below, jnp.logical_not(round_down)))(lambda: z_down(s, y).start())
+        pl.when(round_up)(lambda: relay_up(s, y).start())
+        pl.when(round_down)(lambda: relay_down(s, y).start())
         pl.when(jnp.logical_and(y == 0, before))(lambda: y_down(s).start())
         pl.when(jnp.logical_and(y == ny - 1, after))(lambda: y_up(s).start())
 
@@ -147,6 +180,17 @@
         pl.when(above)(lambda: z_down(s, y).wait_recv())
         pl.when(jnp.logical_and(y == 0, before))(lambda: y_up(s).wait_recv())
         pl.when(jnp.logical_and(y == ny - 1, after))(lambda: y_down(s).wait_recv())
+
+    def forward(s, y):
+        @pl.when(jnp.logical_and(is_last, y < RELAYED))
+        def _():
+            relay_up(s, y + kept).wait_recv()
+            forward_up(s, y + kept).start()
+
+        @pl.when(jnp.logical_and(is_first, y < RELAYED))
+        def _():
+            relay_down(s, y + kept).wait_recv()
+            forward_down(s, y + kept).start()
 
     small = [
         pltpu.make_async_copy(dirs_hbm, dirs, small_sem.at[0]),
@@ -158,9 +202,10 @@
         load(r).start()
 
     barrier = pltpu.get_barrier_semaphore()
-    for there, target in (
-        (below, (gz - 1, gy)), (above, (gz + 1, gy)), (before, (gz, gy - 1)), (after, (gz, gy + 1)),
-    ):
+    inner, outer = jnp.logical_or(is_low, is_high), jnp.logical_or(is_first, is_last)
+    greeted = [(below, (gz - 1, gy)), (above, (gz + 1, gy)), (before, (gz, gy - 1)), (after, (gz, gy + 1))]
+    greeted += [(inner, (0, gy)), (inner, (gz_last, gy)), (outer, (seam_low, gy)), (outer, (seam_high, gy))]
+    for there, target in greeted:
         @pl.when(there)
         def _():
             pl.semaphore_signal(barrier, inc=1, device_id=target, device_id_type=MESH)
@@ -193,7 +238,7 @@
     for c in range(len(rows)):
         coef[c] = jnp.broadcast_to(table[0:HALF, c : c + 1], (HALF, LANES))
 
-    peers = sum(there.astype(jnp.int32) for there in (below, above, before, after))
+    peers = sum(there.astype(jnp.int32) for there, _ in greeted)
     pl.semaphore_wait(barrier, peers)
 
     def first(y, carry):
@@ -264,6 +309,7 @@
 
     def middle(i, carry):
         s, y = i // ny, i % ny
+        forward(s, y)
         advance(s, y, False)
         send(s + 1, y)
         return carry
@@ -271,6 +317,7 @@
     lax.fori_loop(0, (ITERS - 1) * ny, middle, 0)
 
     def final(y, carry):
+        forward(ITERS - 1, y)
         advance(ITERS - 1, y, True)
         for z in range(nz):
             store(y * nz + z).start()
@@ -280,8 +327,9 @@
 
     def sent(i, carry):
         s, y = i // ny, i % ny
-        pl.when(above)(lambda: z_up(s, y).wait_send())
-        pl.when(below)(lambda: z_down(s, y).wait_send())
+        passed = jnp.logical_and(outer, y >= kept)
+        pl.when(jnp.logical_or(above, passed))(lambda: z_up(s, y).wait_send())
+        pl.when(jnp.logical_or(below, passed))(lambda: z_down(s, y).wait_send())
         return carry
 
     lax.fori_loop(0, ITERS * ny, sent, 0)
@@ -299,8 +347,8 @@
     enhanced = pl.pallas_call(
         kernel,
         out_shape=jax.ShapeDtypeStruct(rows.shape, f32),
-        in_specs=[pl.BlockSpec(memory_space=pl.ANY)] * 3,
-        out_specs=pl.BlockSpec(memory_space=pl.ANY),
+        in_specs=[pl.BlockSpec(memory_space=pltpu.HBM)] * 3,
+        out_specs=pl.BlockSpec(memory_space=pltpu.HBM),
         scratch_shapes=[
             vmem((ny * nz, orientations, LANES), f32),
             vmem((3, orientations), f32),
@@ -317,15 +365,17 @@
             vmem((ITERS, nz + 1, ny, HALF, LANES), f32),
             vmem((ITERS, nz, ny + 1, HALF, LANES), f32),
             vmem((ITERS, nz, ny + 1, HALF, LANES), f32),
+            vmem((ITERS, RELAYED, HALF, LANES), f32),
             dma((ny * nz,)),
             dma((2,)),
             dma((2, ITERS, ny)),
             dma((2, ITERS, ny)),
             dma((2, ITERS)),
             dma((2, ITERS)),
+            dma((ITERS, RELAYED)),
         ],
         compiler_params=pltpu.CompilerParams(
-            collective_id=0, has_side_effects=True, vmem_limit_bytes=48 * 1024 * 1024
+            collective_id=0, has_side_effects=True, vmem_limit_bytes=60 * 1024 * 1024
         ),
     )(rows, directions, signs)
     return enhanced.reshape(fodf.shape)

time: 57.8 us -> 64 us (1.11)
  the two profiles are of different devices: /device:TPU:160 before, /device:TPU:32 now
where the time goes in v2:
time: 64 us; the launch traced here: 63.8 us
  Pallas kernels  60.7 us (95%)
  local copies, waits for them, and re-layouts  3.09 us (5%)
    pallas_call x1, Pallas kernels, shards(): pl.pallas_call(kernel, out_shape=jax.ShapeDtypeStruct(rows.shape, f32), i...  60.7 us
    unnamed x1, local copies, waits for them, and re-layouts  3.09 us

profile of v2, /device:TPU:32, one launch (start us, length us, event | category | flops | bytes accessed | tf_op | source)
XLA Modules:
  0.0 63.8 jit_solution(12221441439831141777)
XLA Ops:
  0.0 60.7 %shard_map.37 = f32[192,16,1,128]{3,2,1,0:T(1,128)} custom-call(f32[192,16,1,128]{3,2,1,0:T(1,128)} %bitcast.3, f32[3,192]{1,0:T(4,128)} %dirs_hbm.1, s32[3,192]{1,0:T(4,128)} %signs_hbm.1), custom_call_target="tpu_custom_call" | custom-call | tf_op jit(solution)/shard_map/pallas_call | solution.py:347
  60.7 3.1 %copy.5 = f32[192,8,2,128]{3,2,1,0:T(2,128)} copy(f32[192,8,2,128]{3,2,1,0:T(2,128)} %bitcast.2) | data formatting | bytes 3145728

commit v3 on v2

--- a/solution.py
+++ b/solution.py
@@ -114,9 +114,6 @@
     def load(r):
         return pltpu.make_async_copy(fodf.at[:, r, 0, :], stage.at[r], in_sem.at[r])
 
-    def store(r):
-        return pltpu.make_async_copy(stage.at[r], out.at[:, r, 0, :], in_sem.at[r])
-
     def z_up(s, y):
         return pltpu.make_async_remote_copy(
             p.at[s, nz, y], p.at[s, 0, y], z_send.at[0, s, y], z_recv.at[0, s, y],
@@ -132,24 +129,24 @@
     def relay_up(s, y):
         return pltpu.make_async_remote_copy(
             p.at[s, nz, y], relay.at[s, y - kept], z_send.at[0, s, y], relay_recv.at[s, y - kept],
+            device_id=(0, gy), device_id_type=MESH,
+        )
+
+    def relay_down(s, y):
+        return pltpu.make_async_remote_copy(
+            q.at[s, 0, y], relay.at[s, y - kept], z_send.at[1, s, y], relay_recv.at[s, y - kept],
             device_id=(gz_last, gy), device_id_type=MESH,
         )
 
-    def relay_down(s, y):
-        return pltpu.make_async_remote_copy(
-            q.at[s, 0, y], relay.at[s, y - kept], z_send.at[1, s, y], relay_recv.at[s, y - kept],
-            device_id=(0, gy), device_id_type=MESH,
-        )
-
     def forward_up(s, y):
         return pltpu.make_async_remote_copy(
-            relay.at[s, y - kept], p.at[s, 0, y], z_send.at[0, s, y], z_recv.at[0, s, y],
+            relay.at[s, y - kept], p.at[s, 0, y], z_send.at[1, s, y], z_recv.at[0, s, y],
             device_id=(seam_high, gy), device_id_type=MESH,
         )
 
     def forward_down(s, y):
         return pltpu.make_async_remote_copy(
-            relay.at[s, y - kept], q.at[s, nz, y], z_send.at[1, s, y], z_recv.at[1, s, y],
+            relay.at[s, y - kept], q.at[s, nz, y], z_send.at[0, s, y], z_recv.at[1, s, y],
             device_id=(seam_low, gy), device_id_type=MESH,
         )
 
@@ -182,12 +179,12 @@
         pl.when(jnp.logical_and(y == ny - 1, after))(lambda: y_down(s).wait_recv())
 
     def forward(s, y):
-        @pl.when(jnp.logical_and(is_last, y < RELAYED))
+        @pl.when(jnp.logical_and(is_first, y < RELAYED))
         def _():
             relay_up(s, y + kept).wait_recv()
             forward_up(s, y + kept).start()
 
-        @pl.when(jnp.logical_and(is_first, y < RELAYED))
+        @pl.when(jnp.logical_and(is_last, y < RELAYED))
         def _():
             relay_down(s, y + kept).wait_recv()
             forward_down(s, y + kept).start()
@@ -299,8 +296,9 @@
                 if last:
                     r = y * nz + z
                     upward = coef[SZ, lines] > 0
-                    stage[r, c : c + CHUNK, :] = jnp.where(upward, new_up, new_down)
-                    stage[r, HALF + c : HALF + c + CHUNK, :] = jnp.where(upward, new_down, new_up)
+                    one, other = jnp.where(upward, new_up, new_down), jnp.where(upward, new_down, new_up)
+                    out[pl.ds(c * ny * nz + r, CHUNK, stride=ny * nz), :] = one
+                    out[pl.ds((HALF + c) * ny * nz + r, CHUNK, stride=ny * nz), :] = other
                 else:
                     p[s + 1, z + 1, y, lines] = new_up
                     q[s + 1, z, y, lines] = new_down
@@ -319,8 +317,6 @@
     def final(y, carry):
         forward(ITERS - 1, y)
         advance(ITERS - 1, y, True)
-        for z in range(nz):
-            store(y * nz + z).start()
         return carry
 
     lax.fori_loop(0, ny, final, 0)
@@ -336,8 +332,6 @@
     for s in range(ITERS):
         pl.when(after)(lambda: y_up(s).wait_send())
         pl.when(before)(lambda: y_down(s).wait_send())
-    for r in range(ny * nz):
-        store(r).wait()
 
 
 def shards(fodf, directions, signs):
@@ -346,9 +340,9 @@
     rows = fodf.reshape(orientations, ny * nz, 1, LANES)
     enhanced = pl.pallas_call(
         kernel,
-        out_shape=jax.ShapeDtypeStruct(rows.shape, f32),
+        out_shape=vmem((orientations * ny * nz, LANES), f32),
         in_specs=[pl.BlockSpec(memory_space=pltpu.HBM)] * 3,
-        out_specs=pl.BlockSpec(memory_space=pltpu.HBM),
+        out_specs=pl.BlockSpec(memory_space=vmem),
         scratch_shapes=[
             vmem((ny * nz, orientations, LANES), f32),
             vmem((3, orientations), f32),
@@ -375,9 +369,9 @@
             dma((ITERS, RELAYED)),
         ],
         compiler_params=pltpu.CompilerParams(
-            collective_id=0, has_side_effects=True, vmem_limit_bytes=60 * 1024 * 1024
+            collective_id=0, has_side_effects=True, vmem_limit_bytes=48 * 1024 * 1024
         ),
-    )(rows, directions, signs)
+    )(*(pltpu.with_memory_space_constraint(a, pltpu.HBM) for a in (rows, directions, signs)))
     return enhanced.reshape(fodf.shape)
 
 

time: 64 us -> 50.8 us (0.79)
  the two profiles are of different devices: /device:TPU:32 before, /device:TPU:160 now
where the time goes in v3:
time: 50.8 us; the launch traced here: 50.7 us
  Pallas kernels  49.5 us (97%)
  local copies, waits for them, and re-layouts  1.15 us (2%)
    pallas_call x1, Pallas kernels, shards(): pl.pallas_call(kernel, out_shape=vmem((orientations * ny * nz, LANES), f3...  49.5 us
    unnamed x1, local copies, waits for them, and re-layouts  1.15 us

profile of v3, /device:TPU:160, one launch (start us, length us, event | category | flops | bytes accessed | tf_op | source)
XLA Modules:
  0.0 50.7 jit_solution(12554469622599597535)
XLA Ops:
  0.0 49.5 %shard_map.37 = f32[3072,128]{1,0:T(8,128)S(1)} custom-call(f32[192,16,1,128]{3,2,1,0:T(1,128)} %bitcast.3, f32[3,192]{1,0:T(4,128)} %dirs_hbm.1, s32[3,192]{1,0:T(4,128)} %signs_hbm.1), custom_call_target="tpu_custom_call" | custom-call | tf_op jit(solution)/shard_map/pallas_call | solution.py:341
  49.5 1.1 %copy.5 = f32[192,8,2,128]{3,2,1,0:T(2,128)} copy(f32[192,8,2,128]{3,2,1,0:T(2,128)S(1)} %bitcast.2) | data formatting | bytes 3145728

commit v4 on v3

--- a/solution.py
+++ b/solution.py
@@ -103,6 +103,10 @@
 ):
     ny, nz = p.shape[2], u.shape[1]
     kept = ny - RELAYED
+
+    def row_at(i):
+        return (i + ny - 1) % ny
+
     gz, gy = lax.axis_index("gz"), lax.axis_index("gy")
     gz_last, gy_last = lax.axis_size("gz") - 1, lax.axis_size("gy") - 1
     below, above = gz > 0, gz < gz_last
@@ -126,27 +130,27 @@
             device_id=(gz - 1, gy), device_id_type=MESH,
         )
 
-    def relay_up(s, y):
-        return pltpu.make_async_remote_copy(
-            p.at[s, nz, y], relay.at[s, y - kept], z_send.at[0, s, y], relay_recv.at[s, y - kept],
+    def relay_up(s, i):
+        return pltpu.make_async_remote_copy(
+            p.at[s, nz, row_at(i)], relay.at[s, i - kept], z_send.at[0, s, row_at(i)], relay_recv.at[s, i - kept],
             device_id=(0, gy), device_id_type=MESH,
         )
 
-    def relay_down(s, y):
-        return pltpu.make_async_remote_copy(
-            q.at[s, 0, y], relay.at[s, y - kept], z_send.at[1, s, y], relay_recv.at[s, y - kept],
+    def relay_down(s, i):
+        return pltpu.make_async_remote_copy(
+            q.at[s, 0, row_at(i)], relay.at[s, i - kept], z_send.at[1, s, row_at(i)], relay_recv.at[s, i - kept],
             device_id=(gz_last, gy), device_id_type=MESH,
         )
 
-    def forward_up(s, y):
-        return pltpu.make_async_remote_copy(
-            relay.at[s, y - kept], p.at[s, 0, y], z_send.at[1, s, y], z_recv.at[0, s, y],
+    def forward_up(s, i):
+        return pltpu.make_async_remote_copy(
+            relay.at[s, i - kept], p.at[s, 0, row_at(i)], z_send.at[1, s, row_at(i)], z_recv.at[0, s, row_at(i)],
             device_id=(seam_high, gy), device_id_type=MESH,
         )
 
-    def forward_down(s, y):
-        return pltpu.make_async_remote_copy(
-            relay.at[s, y - kept], q.at[s, nz, y], z_send.at[0, s, y], z_recv.at[1, s, y],
+    def forward_down(s, i):
+        return pltpu.make_async_remote_copy(
+            relay.at[s, i - kept], q.at[s, nz, row_at(i)], z_send.at[0, s, row_at(i)], z_recv.at[1, s, row_at(i)],
             device_id=(seam_low, gy), device_id_type=MESH,
         )
 
@@ -162,13 +166,13 @@
             device_id=(gz, gy - 1), device_id_type=MESH,
         )
 
-    def send(s, y):
-        far = y >= kept
+    def send(s, i):
+        y, far = row_at(i), i >= kept
         round_up, round_down = jnp.logical_and(is_low, far), jnp.logical_and(is_high, far)
         pl.when(jnp.logical_and(above, jnp.logical_not(round_up)))(lambda: z_up(s, y).start())
         pl.when(jnp.logical_and(below, jnp.logical_not(round_down)))(lambda: z_down(s, y).start())
-        pl.when(round_up)(lambda: relay_up(s, y).start())
-        pl.when(round_down)(lambda: relay_down(s, y).start())
+        pl.when(round_up)(lambda: relay_up(s, i).start())
+        pl.when(round_down)(lambda: relay_down(s, i).start())
         pl.when(jnp.logical_and(y == 0, before))(lambda: y_down(s).start())
         pl.when(jnp.logical_and(y == ny - 1, after))(lambda: y_up(s).start())
 
@@ -178,16 +182,16 @@
         pl.when(jnp.logical_and(y == 0, before))(lambda: y_up(s).wait_recv())
         pl.when(jnp.logical_and(y == ny - 1, after))(lambda: y_down(s).wait_recv())
 
-    def forward(s, y):
-        @pl.when(jnp.logical_and(is_first, y < RELAYED))
+    def forward(s, i):
+        @pl.when(jnp.logical_and(is_first, i < RELAYED))
         def _():
-            relay_up(s, y + kept).wait_recv()
-            forward_up(s, y + kept).start()
-
-        @pl.when(jnp.logical_and(is_last, y < RELAYED))
+            relay_up(s, i + kept).wait_recv()
+            forward_up(s, i + kept).start()
+
+        @pl.when(jnp.logical_and(is_last, i < RELAYED))
         def _():
-            relay_down(s, y + kept).wait_recv()
-            forward_down(s, y + kept).start()
+            relay_down(s, i + kept).wait_recv()
+            forward_down(s, i + kept).start()
 
     small = [
         pltpu.make_async_copy(dirs_hbm, dirs, small_sem.at[0]),
@@ -195,8 +199,9 @@
     ]
     for copy in small:
         copy.start()
-    for r in range(ny * nz):
-        load(r).start()
+    for i in range(ny):
+        for z in range(nz):
+            load(row_at(i) * nz + z).start()
 
     barrier = pltpu.get_barrier_semaphore()
     inner, outer = jnp.logical_or(is_low, is_high), jnp.logical_or(is_first, is_last)
@@ -238,7 +243,8 @@
     peers = sum(there.astype(jnp.int32) for there, _ in greeted)
     pl.semaphore_wait(barrier, peers)
 
-    def first(y, carry):
+    def first(i, carry):
+        y = row_at(i)
         for z in range(nz):
             r = y * nz + z
             load(r).wait()
@@ -251,7 +257,7 @@
                 q[0, z, y, lines] = down
                 u[0, z, y + 1, lines] = jnp.where(along_y, up, down)
                 v[0, z, y, lines] = jnp.where(along_y, down, up)
-        send(0, y)
+        send(0, i)
         return carry
 
     lax.fori_loop(0, ny, first, 0)
@@ -305,25 +311,25 @@
                     u[s + 1, z, y + 1, lines] = jnp.where(along_y, new_up, new_down)
                     v[s + 1, z, y, lines] = jnp.where(along_y, new_down, new_up)
 
-    def middle(i, carry):
-        s, y = i // ny, i % ny
-        forward(s, y)
-        advance(s, y, False)
-        send(s + 1, y)
+    def middle(n, carry):
+        s, i = n // ny, n % ny
+        forward(s, i)
+        advance(s, row_at(i), False)
+        send(s + 1, i)
         return carry
 
     lax.fori_loop(0, (ITERS - 1) * ny, middle, 0)
 
-    def final(y, carry):
-        forward(ITERS - 1, y)
-        advance(ITERS - 1, y, True)
+    def final(i, carry):
+        forward(ITERS - 1, i)
+        advance(ITERS - 1, row_at(i), True)
         return carry
 
     lax.fori_loop(0, ny, final, 0)
 
-    def sent(i, carry):
-        s, y = i // ny, i % ny
-        passed = jnp.logical_and(outer, y >= kept)
+    def sent(n, carry):
+        s, i = n // ny, n % ny
+        y, passed = row_at(i), jnp.logical_and(outer, i >= kept)
         pl.when(jnp.logical_or(above, passed))(lambda: z_up(s, y).wait_send())
         pl.when(jnp.logical_or(below, passed))(lambda: z_down(s, y).wait_send())
         return carry

time: 50.8 us -> 49 us (0.965); the launches traced: 50.7 us -> 48.1 us
  Pallas kernels: 49.5 us -> 47 us
    pallas_call x1, Pallas kernels: 49.5 us -> 47 us  [shards(): pl.pallas_call(kernel, out_shape=vmem((orientations * ny * nz, LANES), f3...]
where the time goes in v4:
time: 49 us; the launch traced here: 48.1 us
  Pallas kernels  47 us (96%)
  local copies, waits for them, and re-layouts  1.15 us (2%)
    pallas_call x1, Pallas kernels, shards(): pl.pallas_call(kernel, out_shape=vmem((orientations * ny * nz, LANES), f3...  47 us
    unnamed x1, local copies, waits for them, and re-layouts  1.15 us

profile of v4, /device:TPU:160, one launch (start us, length us, event | category | flops | bytes accessed | tf_op | source)
XLA Modules:
  0.0 48.1 jit_solution(12421726151542758304)
XLA Ops:
  0.0 47.0 %shard_map.37 = f32[3072,128]{1,0:T(8,128)S(1)} custom-call(f32[192,16,1,128]{3,2,1,0:T(1,128)} %bitcast.3, f32[3,192]{1,0:T(4,128)} %dirs_hbm.1, s32[3,192]{1,0:T(4,128)} %signs_hbm.1), custom_call_target="tpu_custom_call" | custom-call | tf_op jit(solution)/shard_map/pallas_call | solution.py:347
  47.0 1.1 %copy.5 = f32[192,8,2,128]{3,2,1,0:T(2,128)} copy(f32[192,8,2,128]{3,2,1,0:T(2,128)S(1)} %bitcast.2) | data formatting | bytes 3145728

commit v5 on v4

--- a/solution.py
+++ b/solution.py
@@ -102,7 +102,6 @@
     in_sem, small_sem, z_send, z_recv, y_send, y_recv, relay_recv,
 ):
     ny, nz = p.shape[2], u.shape[1]
-    kept = ny - RELAYED
 
     def row_at(i):
         return (i + ny - 1) % ny
@@ -132,25 +131,25 @@
 
     def relay_up(s, i):
         return pltpu.make_async_remote_copy(
-            p.at[s, nz, row_at(i)], relay.at[s, i - kept], z_send.at[0, s, row_at(i)], relay_recv.at[s, i - kept],
+            p.at[s, nz, row_at(i)], relay.at[s, i], z_send.at[0, s, row_at(i)], relay_recv.at[s, i],
             device_id=(0, gy), device_id_type=MESH,
         )
 
     def relay_down(s, i):
         return pltpu.make_async_remote_copy(
-            q.at[s, 0, row_at(i)], relay.at[s, i - kept], z_send.at[1, s, row_at(i)], relay_recv.at[s, i - kept],
+            q.at[s, 0, row_at(i)], relay.at[s, i], z_send.at[1, s, row_at(i)], relay_recv.at[s, i],
             device_id=(gz_last, gy), device_id_type=MESH,
         )
 
     def forward_up(s, i):
         return pltpu.make_async_remote_copy(
-            relay.at[s, i - kept], p.at[s, 0, row_at(i)], z_send.at[1, s, row_at(i)], z_recv.at[0, s, row_at(i)],
+            relay.at[s, i], p.at[s, 0, row_at(i)], z_send.at[1, s, row_at(i)], z_recv.at[0, s, row_at(i)],
             device_id=(seam_high, gy), device_id_type=MESH,
         )
 
     def forward_down(s, i):
         return pltpu.make_async_remote_copy(
-            relay.at[s, i - kept], q.at[s, nz, row_at(i)], z_send.at[0, s, row_at(i)], z_recv.at[1, s, row_at(i)],
+            relay.at[s, i], q.at[s, nz, row_at(i)], z_send.at[0, s, row_at(i)], z_recv.at[1, s, row_at(i)],
             device_id=(seam_low, gy), device_id_type=MESH,
         )
 
@@ -167,7 +166,7 @@
         )
 
     def send(s, i):
-        y, far = row_at(i), i >= kept
+        y, far = row_at(i), i < RELAYED
         round_up, round_down = jnp.logical_and(is_low, far), jnp.logical_and(is_high, far)
         pl.when(jnp.logical_and(above, jnp.logical_not(round_up)))(lambda: z_up(s, y).start())
         pl.when(jnp.logical_and(below, jnp.logical_not(round_down)))(lambda: z_down(s, y).start())
@@ -183,15 +182,15 @@
         pl.when(jnp.logical_and(y == ny - 1, after))(lambda: y_down(s).wait_recv())
 
     def forward(s, i):
-        @pl.when(jnp.logical_and(is_first, i < RELAYED))
+        @pl.when(is_first)
         def _():
-            relay_up(s, i + kept).wait_recv()
-            forward_up(s, i + kept).start()
-
-        @pl.when(jnp.logical_and(is_last, i < RELAYED))
+            relay_up(s, i).wait_recv()
+            forward_up(s, i).start()
+
+        @pl.when(is_last)
         def _():
-            relay_down(s, i + kept).wait_recv()
-            forward_down(s, i + kept).start()
+            relay_down(s, i).wait_recv()
+            forward_down(s, i).start()
 
     small = [
         pltpu.make_async_copy(dirs_hbm, dirs, small_sem.at[0]),
@@ -313,15 +312,17 @@
 
     def middle(n, carry):
         s, i = n // ny, n % ny
-        forward(s, i)
         advance(s, row_at(i), False)
         send(s + 1, i)
+        late = i - RELAYED
+        pl.when(jnp.logical_and(late >= 0, late < RELAYED))(lambda: forward(s + 1, late))
         return carry
 
+    for i in range(RELAYED):
+        forward(0, i)
     lax.fori_loop(0, (ITERS - 1) * ny, middle, 0)
 
     def final(i, carry):
-        forward(ITERS - 1, i)
         advance(ITERS - 1, row_at(i), True)
         return carry
 
@@ -329,7 +330,7 @@
 
     def sent(n, carry):
         s, i = n // ny, n % ny
-        y, passed = row_at(i), jnp.logical_and(outer, i >= kept)
+        y, passed = row_at(i), jnp.logical_and(outer, i < RELAYED)
         pl.when(jnp.logical_or(above, passed))(lambda: z_up(s, y).wait_send())
         pl.when(jnp.logical_or(below, passed))(lambda: z_down(s, y).wait_send())
         return carry

time: 49 us -> 47.3 us (0.965)
  the two profiles are of different devices: /device:TPU:160 before, /device:TPU:96 now
where the time goes in v5:
time: 47.3 us; the launch traced here: 47.2 us
  Pallas kernels  46 us (97%)
  local copies, waits for them, and re-layouts  1.15 us (2%)
    pallas_call x1, Pallas kernels, shards(): pl.pallas_call(kernel, out_shape=vmem((orientations * ny * nz, LANES), f3...  46 us
    unnamed x1, local copies, waits for them, and re-layouts  1.15 us

profile of v5, /device:TPU:96, one launch (start us, length us, event | category | flops | bytes accessed | tf_op | source)
XLA Modules:
  0.0 47.2 jit_solution(10483237813331569348)
XLA Ops:
  0.0 46.0 %shard_map.37 = f32[3072,128]{1,0:T(8,128)S(1)} custom-call(f32[192,16,1,128]{3,2,1,0:T(1,128)} %bitcast.3, f32[3,192]{1,0:T(4,128)} %dirs_hbm.1, s32[3,192]{1,0:T(4,128)} %signs_hbm.1), custom_call_target="tpu_custom_call" | custom-call | tf_op jit(solution)/shard_map/pallas_call | solution.py:348
  46.0 1.1 %copy.5 = f32[192,8,2,128]{3,2,1,0:T(2,128)} copy(f32[192,8,2,128]{3,2,1,0:T(2,128)S(1)} %bitcast.2) | data formatting | bytes 3145728

commit v6 on v5

--- a/solution.py
+++ b/solution.py
@@ -129,27 +129,30 @@
             device_id=(gz - 1, gy), device_id_type=MESH,
         )
 
+    def is_relayed(s, i):
+        return jnp.where(s == 0, i >= ny - RELAYED, i < RELAYED)
+
     def relay_up(s, i):
         return pltpu.make_async_remote_copy(
-            p.at[s, nz, row_at(i)], relay.at[s, i], z_send.at[0, s, row_at(i)], relay_recv.at[s, i],
+            p.at[s, nz, row_at(i)], relay.at[s, i % (ny - RELAYED)], z_send.at[0, s, row_at(i)], relay_recv.at[s, i % (ny - RELAYED)],
             device_id=(0, gy), device_id_type=MESH,
         )
 
     def relay_down(s, i):
         return pltpu.make_async_remote_copy(
-            q.at[s, 0, row_at(i)], relay.at[s, i], z_send.at[1, s, row_at(i)], relay_recv.at[s, i],
+            q.at[s, 0, row_at(i)], relay.at[s, i % (ny - RELAYED)], z_send.at[1, s, row_at(i)], relay_recv.at[s, i % (ny - RELAYED)],
             device_id=(gz_last, gy), device_id_type=MESH,
         )
 
     def forward_up(s, i):
         return pltpu.make_async_remote_copy(
-            relay.at[s, i], p.at[s, 0, row_at(i)], z_send.at[1, s, row_at(i)], z_recv.at[0, s, row_at(i)],
+            relay.at[s, i % (ny - RELAYED)], p.at[s, 0, row_at(i)], z_send.at[1, s, row_at(i)], z_recv.at[0, s, row_at(i)],
             device_id=(seam_high, gy), device_id_type=MESH,
         )
 
     def forward_down(s, i):
         return pltpu.make_async_remote_copy(
-            relay.at[s, i], q.at[s, nz, row_at(i)], z_send.at[0, s, row_at(i)], z_recv.at[1, s, row_at(i)],
+            relay.at[s, i % (ny - RELAYED)], q.at[s, nz, row_at(i)], z_send.at[0, s, row_at(i)], z_recv.at[1, s, row_at(i)],
             device_id=(seam_low, gy), device_id_type=MESH,
         )
 
@@ -166,7 +169,7 @@
         )
 
     def send(s, i):
-        y, far = row_at(i), i < RELAYED
+        y, far = row_at(i), is_relayed(s, i)
         round_up, round_down = jnp.logical_and(is_low, far), jnp.logical_and(is_high, far)
         pl.when(jnp.logical_and(above, jnp.logical_not(round_up)))(lambda: z_up(s, y).start())
         pl.when(jnp.logical_and(below, jnp.logical_not(round_down)))(lambda: z_down(s, y).start())
@@ -236,8 +239,12 @@
     rows.append(1.0 - (rows[0] + rows[1] + rows[2]))
     rows += [sign[0:1] * sign_z, sign[1:2] * sign_z, sign_z]
     table = jnp.concatenate(rows + [jnp.zeros((LANES - len(rows), LANES), jnp.float32)], 0).T
-    for c in range(len(rows)):
+
+    def spread(c):
         coef[c] = jnp.broadcast_to(table[0:HALF, c : c + 1], (HALF, LANES))
+
+    spread(SZ)
+    spread(SY)
 
     peers = sum(there.astype(jnp.int32) for there, _ in greeted)
     pl.semaphore_wait(barrier, peers)
@@ -260,6 +267,8 @@
         return carry
 
     lax.fori_loop(0, ny, first, 0)
+    for c in (AX, AY, AZ, CENTER, SX):
+        spread(c)
 
     matrix = angular_matrix(dirs, basis, scaled, left, right)[0:HALF, 0:HALF]
     high = matrix.astype(jnp.bfloat16)
@@ -314,31 +323,35 @@
         s, i = n // ny, n % ny
         advance(s, row_at(i), False)
         send(s + 1, i)
-        late = i - RELAYED
+        late = i - 4
         pl.when(jnp.logical_and(late >= 0, late < RELAYED))(lambda: forward(s + 1, late))
         return carry
 
-    for i in range(RELAYED):
+    for i in range(ny - RELAYED, ny):
         forward(0, i)
     lax.fori_loop(0, (ITERS - 1) * ny, middle, 0)
 
+    def sent(s, i):
+        y, passed = row_at(i), jnp.logical_and(outer, is_relayed(s, i))
+        pl.when(jnp.logical_or(above, passed))(lambda: z_up(s, y).wait_send())
+        pl.when(jnp.logical_or(below, passed))(lambda: z_down(s, y).wait_send())
+
+    def y_sent(s):
+        pl.when(after)(lambda: y_up(s).wait_send())
+        pl.when(before)(lambda: y_down(s).wait_send())
+
     def final(i, carry):
+        for s in range(ITERS - 1):
+            sent(s, i)
         advance(ITERS - 1, row_at(i), True)
         return carry
 
+    for s in range(ITERS - 1):
+        y_sent(s)
     lax.fori_loop(0, ny, final, 0)
-
-    def sent(n, carry):
-        s, i = n // ny, n % ny
-        y, passed = row_at(i), jnp.logical_and(outer, i < RELAYED)
-        pl.when(jnp.logical_or(above, passed))(lambda: z_up(s, y).wait_send())
-        pl.when(jnp.logical_or(below, passed))(lambda: z_down(s, y).wait_send())
-        return carry
-
-    lax.fori_loop(0, ITERS * ny, sent, 0)
-    for s in range(ITERS):
-        pl.when(after)(lambda: y_up(s).wait_send())
-        pl.when(before)(lambda: y_down(s).wait_send())
+    for i in range(ny):
+        sent(ITERS - 1, i)
+    y_sent(ITERS - 1)
 
 
 def shards(fodf, directions, signs):

time: 47.3 us -> 45 us (0.951)
  the two profiles are of different devices: /device:TPU:96 before, /device:TPU:160 now
where the time goes in v6:
time: 45 us; the launch traced here: 44.8 us
  Pallas kernels  43.6 us (97%)
  local copies, waits for them, and re-layouts  1.15 us (3%)
    pallas_call x1, Pallas kernels, shards(): pl.pallas_call(kernel, out_shape=vmem((orientations * ny * nz, LANES), f3...  43.6 us
    unnamed x1, local copies, waits for them, and re-layouts  1.15 us

profile of v6, /device:TPU:160, one launch (start us, length us, event | category | flops | bytes accessed | tf_op | source)
XLA Modules:
  0.0 44.8 jit_solution(1108851494326843298)
XLA Ops:
  0.0 43.6 %shard_map.37 = f32[3072,128]{1,0:T(8,128)S(1)} custom-call(f32[192,16,1,128]{3,2,1,0:T(1,128)} %bitcast.3, f32[3,192]{1,0:T(4,128)} %dirs_hbm.1, s32[3,192]{1,0:T(4,128)} %signs_hbm.1), custom_call_target="tpu_custom_call" | custom-call | tf_op jit(solution)/shard_map/pallas_call | solution.py:361
  43.6 1.1 %copy.5 = f32[192,8,2,128]{3,2,1,0:T(2,128)} copy(f32[192,8,2,128]{3,2,1,0:T(2,128)S(1)} %bitcast.2) | data formatting | bytes 3145728

commit v7 on v6

--- a/solution.py
+++ b/solution.py
@@ -17,7 +17,8 @@
 MODES = 45
 MODES_PAD = 48
 CHUNK = 16
-RELAYED = 3
+LAG = 4
+RELAYED = 4
 HIGHEST = lax.Precision.HIGHEST
 MESH = pl.DeviceIdType.MESH
 
@@ -129,30 +130,27 @@
             device_id=(gz - 1, gy), device_id_type=MESH,
         )
 
-    def is_relayed(s, i):
-        return jnp.where(s == 0, i >= ny - RELAYED, i < RELAYED)
-
     def relay_up(s, i):
         return pltpu.make_async_remote_copy(
-            p.at[s, nz, row_at(i)], relay.at[s, i % (ny - RELAYED)], z_send.at[0, s, row_at(i)], relay_recv.at[s, i % (ny - RELAYED)],
+            p.at[s, nz, row_at(i)], relay.at[s, i], z_send.at[0, s, row_at(i)], relay_recv.at[s, i],
             device_id=(0, gy), device_id_type=MESH,
         )
 
     def relay_down(s, i):
         return pltpu.make_async_remote_copy(
-            q.at[s, 0, row_at(i)], relay.at[s, i % (ny - RELAYED)], z_send.at[1, s, row_at(i)], relay_recv.at[s, i % (ny - RELAYED)],
+            q.at[s, 0, row_at(i)], relay.at[s, i], z_send.at[1, s, row_at(i)], relay_recv.at[s, i],
             device_id=(gz_last, gy), device_id_type=MESH,
         )
 
     def forward_up(s, i):
         return pltpu.make_async_remote_copy(
-            relay.at[s, i % (ny - RELAYED)], p.at[s, 0, row_at(i)], z_send.at[1, s, row_at(i)], z_recv.at[0, s, row_at(i)],
+            relay.at[s, i], p.at[s, 0, row_at(i)], z_send.at[1, s, row_at(i)], z_recv.at[0, s, row_at(i)],
             device_id=(seam_high, gy), device_id_type=MESH,
         )
 
     def forward_down(s, i):
         return pltpu.make_async_remote_copy(
-            relay.at[s, i % (ny - RELAYED)], q.at[s, nz, row_at(i)], z_send.at[0, s, row_at(i)], z_recv.at[1, s, row_at(i)],
+            relay.at[s, i], q.at[s, nz, row_at(i)], z_send.at[0, s, row_at(i)], z_recv.at[1, s, row_at(i)],
             device_id=(seam_low, gy), device_id_type=MESH,
         )
 
@@ -168,19 +166,23 @@
             device_id=(gz, gy - 1), device_id_type=MESH,
         )
 
-    def send(s, i):
-        y, far = row_at(i), is_relayed(s, i)
+    def send_z(s, i):
+        y, far = row_at(i), i < RELAYED
         round_up, round_down = jnp.logical_and(is_low, far), jnp.logical_and(is_high, far)
         pl.when(jnp.logical_and(above, jnp.logical_not(round_up)))(lambda: z_up(s, y).start())
         pl.when(jnp.logical_and(below, jnp.logical_not(round_down)))(lambda: z_down(s, y).start())
         pl.when(round_up)(lambda: relay_up(s, i).start())
         pl.when(round_down)(lambda: relay_down(s, i).start())
+
+    def send_y(s, y):
         pl.when(jnp.logical_and(y == 0, before))(lambda: y_down(s).start())
         pl.when(jnp.logical_and(y == ny - 1, after))(lambda: y_up(s).start())
 
-    def receive(s, y):
+    def receive_z(s, y):
         pl.when(below)(lambda: z_up(s, y).wait_recv())
         pl.when(above)(lambda: z_down(s, y).wait_recv())
+
+    def receive_y(s, y):
         pl.when(jnp.logical_and(y == 0, before))(lambda: y_up(s).wait_recv())
         pl.when(jnp.logical_and(y == ny - 1, after))(lambda: y_down(s).wait_recv())
 
@@ -216,11 +218,11 @@
 
     @pl.when(gz == 0)
     def _():
-        p[:, 0] = jnp.zeros_like(p[:, 0])
+        p[0:ITERS, 0] = jnp.zeros_like(p[0:ITERS, 0])
 
     @pl.when(gz == gz_last)
     def _():
-        q[:, nz] = jnp.zeros_like(q[:, nz])
+        q[0:ITERS, nz] = jnp.zeros_like(q[0:ITERS, nz])
 
     @pl.when(gy == 0)
     def _():
@@ -263,7 +265,8 @@
                 q[0, z, y, lines] = down
                 u[0, z, y + 1, lines] = jnp.where(along_y, up, down)
                 v[0, z, y, lines] = jnp.where(along_y, down, up)
-        send(0, i)
+        send_z(0, i)
+        send_y(0, y)
         return carry
 
     lax.fori_loop(0, ny, first, 0)
@@ -277,7 +280,8 @@
 
     lane = lax.broadcasted_iota(jnp.int32, (CHUNK, LANES), 1)
 
-    def advance(s, y, last):
+    def local(s, y):
+        receive_y(s, y)
         total = jnp.concatenate([p[s, z + 1, y] + q[s, z, y] for z in range(nz)], 1)
         total_hi = total.astype(jnp.bfloat16)
         total_lo = (total - total_hi.astype(jnp.float32)).astype(jnp.bfloat16)
@@ -287,7 +291,6 @@
             + jnp.dot(hi, total_lo, preferred_element_type=jnp.float32)
             + jnp.dot(lo, total_hi, preferred_element_type=jnp.float32)
         )
-        receive(s, y)
         for z in range(nz):
             for c in range(0, HALF, CHUNK):
                 lines = slice(c, c + CHUNK)
@@ -301,38 +304,47 @@
                 ax, ay, az, center = (coef[i, lines] for i in (AX, AY, AZ, CENTER))
                 new_up = (
                     center * up + ang + ax * jnp.where(along_x, rising, falling)
-                    + ay * jnp.where(along_y, y_low, y_high) + az * p[s, z, y, lines]
+                    + ay * jnp.where(along_y, y_low, y_high)
                 )
                 new_down = (
                     center * down + ang + ax * jnp.where(along_x, falling, rising)
-                    + ay * jnp.where(along_y, y_high, y_low) + az * q[s, z + 1, y, lines]
+                    + ay * jnp.where(along_y, y_high, y_low)
                 )
+                if z > 0:
+                    new_up += az * p[s, z, y, lines]
+                if z < nz - 1:
+                    new_down += az * q[s, z + 1, y, lines]
+                p[s + 1, z + 1, y, lines] = new_up
+                q[s + 1, z, y, lines] = new_down
+
+    def finish(s, y, last):
+        receive_z(s, y)
+        for c in range(0, HALF, CHUNK):
+            lines = slice(c, c + CHUNK)
+            az = coef[AZ, lines]
+            for z in range(nz):
+                up, down = p[s + 1, z + 1, y, lines], q[s + 1, z, y, lines]
+                if z == 0:
+                    up += az * p[s, 0, y, lines]
+                if z == nz - 1:
+                    down += az * q[s, nz, y, lines]
                 if last:
                     r = y * nz + z
                     upward = coef[SZ, lines] > 0
-                    one, other = jnp.where(upward, new_up, new_down), jnp.where(upward, new_down, new_up)
+                    one, other = jnp.where(upward, up, down), jnp.where(upward, down, up)
                     out[pl.ds(c * ny * nz + r, CHUNK, stride=ny * nz), :] = one
                     out[pl.ds((HALF + c) * ny * nz + r, CHUNK, stride=ny * nz), :] = other
                 else:
-                    p[s + 1, z + 1, y, lines] = new_up
-                    q[s + 1, z, y, lines] = new_down
-                    u[s + 1, z, y + 1, lines] = jnp.where(along_y, new_up, new_down)
-                    v[s + 1, z, y, lines] = jnp.where(along_y, new_down, new_up)
-
-    def middle(n, carry):
-        s, i = n // ny, n % ny
-        advance(s, row_at(i), False)
-        send(s + 1, i)
-        late = i - 4
-        pl.when(jnp.logical_and(late >= 0, late < RELAYED))(lambda: forward(s + 1, late))
-        return carry
-
-    for i in range(ny - RELAYED, ny):
-        forward(0, i)
-    lax.fori_loop(0, (ITERS - 1) * ny, middle, 0)
+                    along_y = coef[SY, lines] > 0
+                    if z == 0:
+                        p[s + 1, 1, y, lines] = up
+                    if z == nz - 1:
+                        q[s + 1, nz - 1, y, lines] = down
+                    u[s + 1, z, y + 1, lines] = jnp.where(along_y, up, down)
+                    v[s + 1, z, y, lines] = jnp.where(along_y, down, up)
 
     def sent(s, i):
-        y, passed = row_at(i), jnp.logical_and(outer, is_relayed(s, i))
+        y, passed = row_at(i), jnp.logical_and(outer, i < RELAYED)
         pl.when(jnp.logical_or(above, passed))(lambda: z_up(s, y).wait_send())
         pl.when(jnp.logical_or(below, passed))(lambda: z_down(s, y).wait_send())
 
@@ -340,18 +352,44 @@
         pl.when(after)(lambda: y_up(s).wait_send())
         pl.when(before)(lambda: y_down(s).wait_send())
 
-    def final(i, carry):
+    for i in range(RELAYED):
+        forward(0, i)
+
+    def step(s, carry):
+        def ahead(i, carry):
+            local(s, row_at(i))
+            send_z(s + 1, i)
+            return carry
+
+        def behind(i, carry):
+            finish(s, row_at(i), False)
+            send_y(s + 1, row_at(i))
+            late = i - LAG
+            pl.when(jnp.logical_and(late >= 0, late < RELAYED))(lambda: forward(s + 1, late))
+            return carry
+
+        lax.fori_loop(0, ny, ahead, 0)
+        lax.fori_loop(0, ny, behind, 0)
+        return carry
+
+    lax.fori_loop(0, ITERS - 1, step, 0)
+
+    def ahead(i, carry):
         for s in range(ITERS - 1):
             sent(s, i)
-        advance(ITERS - 1, row_at(i), True)
+        local(ITERS - 1, row_at(i))
         return carry
 
-    for s in range(ITERS - 1):
+    def behind(i, carry):
+        finish(ITERS - 1, row_at(i), True)
+        return carry
+
+    lax.fori_loop(0, ny, ahead, 0)
+    for s in range(ITERS):
         y_sent(s)
-    lax.fori_loop(0, ny, final, 0)
+    lax.fori_loop(0, ny, behind, 0)
     for i in range(ny):
         sent(ITERS - 1, i)
-    y_sent(ITERS - 1)
 
 
 def shards(fodf, directions, signs):
@@ -375,8 +413,8 @@
             vmem((HALF, HALF), jnp.bfloat16),
             vmem((HALF, HALF), jnp.bfloat16),
             vmem((HALF, nz * LANES), f32),
-            vmem((ITERS, nz + 1, ny, HALF, LANES), f32),
-            vmem((ITERS, nz + 1, ny, HALF, LANES), f32),
+            vmem((ITERS + 1, nz + 1, ny, HALF, LANES), f32),
+            vmem((ITERS + 1, nz + 1, ny, HALF, LANES), f32),
             vmem((ITERS, nz, ny + 1, HALF, LANES), f32),
             vmem((ITERS, nz, ny + 1, HALF, LANES), f32),
             vmem((ITERS, RELAYED, HALF, LANES), f32),

time: 45 us -> 43.7 us (0.971)
  the two profiles are of different devices: /device:TPU:160 before, /device:TPU:97 now
where the time goes in v7:
time: 43.7 us; the launch traced here: 43.6 us
  Pallas kernels  42.4 us (97%)
  local copies, waits for them, and re-layouts  1.15 us (3%)
    pallas_call x1, Pallas kernels, shards(): pl.pallas_call(kernel, out_shape=vmem((orientations * ny * nz, LANES), f3...  42.4 us
    unnamed x1, local copies, waits for them, and re-layouts  1.15 us

profile of v7, /device:TPU:97, one launch (start us, length us, event | category | flops | bytes accessed | tf_op | source)
XLA Modules:
  0.0 43.6 jit_solution(1562821526387600093)
XLA Ops:
  0.0 42.4 %shard_map.37 = f32[3072,128]{1,0:T(8,128)S(1)} custom-call(f32[192,16,1,128]{3,2,1,0:T(1,128)} %bitcast.3, f32[3,192]{1,0:T(4,128)} %dirs_hbm.1, s32[3,192]{1,0:T(4,128)} %signs_hbm.1), custom_call_target="tpu_custom_call" | custom-call | tf_op jit(solution)/shard_map/pallas_call | solution.py:399
  42.4 1.1 %copy.5 = f32[192,8,2,128]{3,2,1,0:T(2,128)} copy(f32[192,8,2,128]{3,2,1,0:T(2,128)S(1)} %bitcast.2) | data formatting | bytes 3145728

commit v8 on v7

--- a/solution.py
+++ b/solution.py
@@ -17,8 +17,8 @@
 MODES = 45
 MODES_PAD = 48
 CHUNK = 16
-LAG = 4
-RELAYED = 4
+ROWS = 2
+RELAYED = 2
 HIGHEST = lax.Precision.HIGHEST
 MESH = pl.DeviceIdType.MESH
 
@@ -104,9 +104,7 @@
 ):
     ny, nz = p.shape[2], u.shape[1]
 
-    def row_at(i):
-        return (i + ny - 1) % ny
-
+    blocks = ny // ROWS
     gz, gy = lax.axis_index("gz"), lax.axis_index("gy")
     gz_last, gy_last = lax.axis_size("gz") - 1, lax.axis_size("gy") - 1
     below, above = gz > 0, gz < gz_last
@@ -118,39 +116,39 @@
     def load(r):
         return pltpu.make_async_copy(fodf.at[:, r, 0, :], stage.at[r], in_sem.at[r])
 
-    def z_up(s, y):
-        return pltpu.make_async_remote_copy(
-            p.at[s, nz, y], p.at[s, 0, y], z_send.at[0, s, y], z_recv.at[0, s, y],
+    def z_up(s, i):
+        return pltpu.make_async_remote_copy(
+            p.at[s, nz, pl.ds(i * ROWS, ROWS)], p.at[s, 0, pl.ds(i * ROWS, ROWS)], z_send.at[0, s, i], z_recv.at[0, s, i],
             device_id=(gz + 1, gy), device_id_type=MESH,
         )
 
-    def z_down(s, y):
-        return pltpu.make_async_remote_copy(
-            q.at[s, 0, y], q.at[s, nz, y], z_send.at[1, s, y], z_recv.at[1, s, y],
+    def z_down(s, i):
+        return pltpu.make_async_remote_copy(
+            q.at[s, 0, pl.ds(i * ROWS, ROWS)], q.at[s, nz, pl.ds(i * ROWS, ROWS)], z_send.at[1, s, i], z_recv.at[1, s, i],
             device_id=(gz - 1, gy), device_id_type=MESH,
         )
 
     def relay_up(s, i):
         return pltpu.make_async_remote_copy(
-            p.at[s, nz, row_at(i)], relay.at[s, i], z_send.at[0, s, row_at(i)], relay_recv.at[s, i],
+            p.at[s, nz, pl.ds(i * ROWS, ROWS)], relay.at[s, i], z_send.at[0, s, i], relay_recv.at[s, i],
             device_id=(0, gy), device_id_type=MESH,
         )
 
     def relay_down(s, i):
         return pltpu.make_async_remote_copy(
-            q.at[s, 0, row_at(i)], relay.at[s, i], z_send.at[1, s, row_at(i)], relay_recv.at[s, i],
+            q.at[s, 0, pl.ds(i * ROWS, ROWS)], relay.at[s, i], z_send.at[1, s, i], relay_recv.at[s, i],
             device_id=(gz_last, gy), device_id_type=MESH,
         )
 
     def forward_up(s, i):
         return pltpu.make_async_remote_copy(
-            relay.at[s, i], p.at[s, 0, row_at(i)], z_send.at[1, s, row_at(i)], z_recv.at[0, s, row_at(i)],
+            relay.at[s, i], p.at[s, 0, pl.ds(i * ROWS, ROWS)], z_send.at[1, s, i], z_recv.at[0, s, i],
             device_id=(seam_high, gy), device_id_type=MESH,
         )
 
     def forward_down(s, i):
         return pltpu.make_async_remote_copy(
-            relay.at[s, i], q.at[s, nz, row_at(i)], z_send.at[0, s, row_at(i)], z_recv.at[1, s, row_at(i)],
+            relay.at[s, i], q.at[s, nz, pl.ds(i * ROWS, ROWS)], z_send.at[0, s, i], z_recv.at[1, s, i],
             device_id=(seam_low, gy), device_id_type=MESH,
         )
 
@@ -167,10 +165,10 @@
         )
 
     def send_z(s, i):
-        y, far = row_at(i), i < RELAYED
+        far = i < RELAYED
         round_up, round_down = jnp.logical_and(is_low, far), jnp.logical_and(is_high, far)
-        pl.when(jnp.logical_and(above, jnp.logical_not(round_up)))(lambda: z_up(s, y).start())
-        pl.when(jnp.logical_and(below, jnp.logical_not(round_down)))(lambda: z_down(s, y).start())
+        pl.when(jnp.logical_and(above, jnp.logical_not(round_up)))(lambda: z_up(s, i).start())
+        pl.when(jnp.logical_and(below, jnp.logical_not(round_down)))(lambda: z_down(s, i).start())
         pl.when(round_up)(lambda: relay_up(s, i).start())
         pl.when(round_down)(lambda: relay_down(s, i).start())
 
@@ -178,9 +176,9 @@
         pl.when(jnp.logical_and(y == 0, before))(lambda: y_down(s).start())
         pl.when(jnp.logical_and(y == ny - 1, after))(lambda: y_up(s).start())
 
-    def receive_z(s, y):
-        pl.when(below)(lambda: z_up(s, y).wait_recv())
-        pl.when(above)(lambda: z_down(s, y).wait_recv())
+    def receive_z(s, i):
+        pl.when(below)(lambda: z_up(s, i).wait_recv())
+        pl.when(above)(lambda: z_down(s, i).wait_recv())
 
     def receive_y(s, y):
         pl.when(jnp.logical_and(y == 0, before))(lambda: y_up(s).wait_recv())
@@ -205,7 +203,7 @@
         copy.start()
     for i in range(ny):
         for z in range(nz):
-            load(row_at(i) * nz + z).start()
+            load(i * nz + z).start()
 
     barrier = pltpu.get_barrier_semaphore()
     inner, outer = jnp.logical_or(is_low, is_high), jnp.logical_or(is_first, is_last)
@@ -252,7 +250,7 @@
     pl.semaphore_wait(barrier, peers)
 
     def first(i, carry):
-        y = row_at(i)
+        y = i
         for z in range(nz):
             r = y * nz + z
             load(r).wait()
@@ -265,7 +263,7 @@
                 q[0, z, y, lines] = down
                 u[0, z, y + 1, lines] = jnp.where(along_y, up, down)
                 v[0, z, y, lines] = jnp.where(along_y, down, up)
-        send_z(0, i)
+        pl.when(i % ROWS == ROWS - 1)(lambda: send_z(0, i // ROWS))
         send_y(0, y)
         return carry
 
@@ -318,7 +316,7 @@
                 q[s + 1, z, y, lines] = new_down
 
     def finish(s, y, last):
-        receive_z(s, y)
+        pl.when(y % ROWS == 0)(lambda: receive_z(s, y // ROWS))
         for c in range(0, HALF, CHUNK):
             lines = slice(c, c + CHUNK)
             az = coef[AZ, lines]
@@ -344,9 +342,9 @@
                     v[s + 1, z, y, lines] = jnp.where(along_y, down, up)
 
     def sent(s, i):
-        y, passed = row_at(i), jnp.logical_and(outer, i < RELAYED)
-        pl.when(jnp.logical_or(above, passed))(lambda: z_up(s, y).wait_send())
-        pl.when(jnp.logical_or(below, passed))(lambda: z_down(s, y).wait_send())
+        passed = jnp.logical_and(outer, i < RELAYED)
+        pl.when(jnp.logical_or(above, passed))(lambda: z_up(s, i).wait_send())
+        pl.when(jnp.logical_or(below, passed))(lambda: z_down(s, i).wait_send())
 
     def y_sent(s):
         pl.when(after)(lambda: y_up(s).wait_send())
@@ -357,38 +355,38 @@
 
     def step(s, carry):
         def ahead(i, carry):
-            local(s, row_at(i))
-            send_z(s + 1, i)
+            local(s, i)
+            pl.when(i % ROWS == ROWS - 1)(lambda: send_z(s + 1, i // ROWS))
             return carry
 
         def behind(i, carry):
-            finish(s, row_at(i), False)
-            send_y(s + 1, row_at(i))
-            late = i - LAG
-            pl.when(jnp.logical_and(late >= 0, late < RELAYED))(lambda: forward(s + 1, late))
+            finish(s, i, False)
+            send_y(s + 1, i)
             return carry
 
         lax.fori_loop(0, ny, ahead, 0)
         lax.fori_loop(0, ny, behind, 0)
+        for i in range(RELAYED):
+            forward(s + 1, i)
         return carry
 
     lax.fori_loop(0, ITERS - 1, step, 0)
 
     def ahead(i, carry):
         for s in range(ITERS - 1):
-            sent(s, i)
-        local(ITERS - 1, row_at(i))
+            pl.when(i < blocks)(lambda s=s: sent(s, i))
+        local(ITERS - 1, i)
         return carry
 
     def behind(i, carry):
-        finish(ITERS - 1, row_at(i), True)
+        finish(ITERS - 1, i, True)
         return carry
 
     lax.fori_loop(0, ny, ahead, 0)
     for s in range(ITERS):
         y_sent(s)
     lax.fori_loop(0, ny, behind, 0)
-    for i in range(ny):
+    for i in range(blocks):
         sent(ITERS - 1, i)
 
 
@@ -417,11 +415,11 @@
             vmem((ITERS + 1, nz + 1, ny, HALF, LANES), f32),
             vmem((ITERS, nz, ny + 1, HALF, LANES), f32),
             vmem((ITERS, nz, ny + 1, HALF, LANES), f32),
-            vmem((ITERS, RELAYED, HALF, LANES), f32),
+            vmem((ITERS, RELAYED, ROWS, HALF, LANES), f32),
             dma((ny * nz,)),
             dma((2,)),
-            dma((2, ITERS, ny)),
-            dma((2, ITERS, ny)),
+            dma((2, ITERS, ny // ROWS)),
+            dma((2, ITERS, ny // ROWS)),
             dma((2, ITERS)),
             dma((2, ITERS)),
             dma((ITERS, RELAYED)),

time: 43.7 us -> 43 us (0.984)
  the two profiles are of different devices: /device:TPU:97 before, /device:TPU:162 now
where the time goes in v8:
time: 43 us; the launch traced here: 42.9 us
  Pallas kernels  41.7 us (97%)
  local copies, waits for them, and re-layouts  1.15 us (3%)
    pallas_call x1, Pallas kernels, shards(): pl.pallas_call(kernel, out_shape=vmem((orientations * ny * nz, LANES), f3...  41.7 us
    unnamed x1, local copies, waits for them, and re-layouts  1.15 us

profile of v8, /device:TPU:162, one launch (start us, length us, event | category | flops | bytes accessed | tf_op | source)
XLA Modules:
  0.0 42.9 jit_solution(4253815009743800576)
XLA Ops:
  0.0 41.7 %shard_map.37 = f32[3072,128]{1,0:T(8,128)S(1)} custom-call(f32[192,16,1,128]{3,2,1,0:T(1,128)} %bitcast.3, f32[3,192]{1,0:T(4,128)} %dirs_hbm.1, s32[3,192]{1,0:T(4,128)} %signs_hbm.1), custom_call_target="tpu_custom_call" | custom-call | tf_op jit(solution)/shard_map/pallas_call | solution.py:397
  41.7 1.1 %copy.5 = f32[192,8,2,128]{3,2,1,0:T(2,128)} copy(f32[192,8,2,128]{3,2,1,0:T(2,128)S(1)} %bitcast.2) | data formatting | bytes 3145728
